TPU v7x, 32 devices: a whole 2x2x4 slice. The times are simulated.
32 devices in a mesh: req: 8 (over z, x), tp: 4 (over y, core).
Axes of the slice: x: 2, y: 2, z: 4, core: 2. Of those that a mesh axis runs over, the one named last changes fastest.
Arguments:
- queries: bfloat16 [4, 256, 8192], P(None, 'req', 'tp'), may hold values from -8 to 8
- new_kv: bfloat16 [4, 256, 2, 1024], P(None, 'req', None, 'tp'), may hold values from -8 to 8
- prefill_page_pool: bfloat16 [2048, 2, 16, 1024], P('req', None, None, 'tp'), may hold values from -6 to 6
- page_table: int32 [256, 8], P('req'), may hold values from 0 to 255, as said below
- prompt_len: int32 [256], P('req'), may hold values from 1 to 128
- dest_device: int32 [256], P('req'), may hold values from 0 to 7, as said below
- ssm_state: float32 [256, 16, 16384], P('req', None, 'tp'), may hold values from -4 to 4
- conv_state: bfloat16 [256, 3, 16384], P('req', None, 'tp'), may hold values from -6 to 6
- mamba_x: bfloat16 [4, 256, 16384], P(None, 'req', 'tp'), may hold values from -6 to 6
- mamba_z: bfloat16 [4, 256, 16384], P(None, 'req', 'tp'), may hold values from -6 to 6
- conv_weight: float32 [4, 16384], P(None, 'tp'), may hold values from -3 to 3
- conv_bias: float32 [16384], P('tp'), may hold values from -0.5 to 0.5
- x_proj: bfloat16 [16384, 544], P('tp'), may hold values from -0.046875 to 0.046875
- dt_gain: float32 [512], replicated, may hold values from 0.25 to 1.75
- dt_proj: bfloat16 [512, 16384], P(None, 'tp'), may hold values from -0.25 to 0.25
- dt_bias: float32 [16384], P('tp'), may hold values from -3 to 0
- a_log: float32 [16, 16384], P(None, 'tp'), may hold values from -1 to 2.8
- skip_d: float32 [16384], P('tp'), may hold values from 0.5 to 1.5
Outputs:
- attn_out: bfloat16 [4, 256, 8192], P(None, 'req', 'tp')
- mamba_out: bfloat16 [4, 256, 16384], P(None, 'req', 'tp')
Inputs may be any that keep to these rules, and one draw needn't show every extreme that they name: `dest_device`: each prefill device hands exactly 4 of its requests to every decode device. `page_table`: the entries of one prefill device's rows are distinct pages of its own pool; only the first ceil(prompt_len / 16) of a row hold the request's tokens.
All inputs are finite; a program needn't handle non-finite values.
Results may differ from a plain program's by a relative error of at most 0.01.
Values may be sent and summed in bfloat16 or wider, within the bound.
A program may use at most 128 MiB of HBM per device.

v0:
```python
import math

import jax
import jax.numpy as jnp
from jax import lax
from jax.sharding import PartitionSpec as P

HEAD_SIZE = 128


EPSILON = 1e-06
HIGHEST = lax.Precision.HIGHEST


def cached_part(grouped, cache_keys, cache_values, key_valid, score_scale):
    scores = (
        jnp.einsum("trkgd,rskd->trkgs", grouped, cache_keys, preferred_element_type=jnp.float32)
        * score_scale
    )
    scores = jnp.where(key_valid[None, :, None, None, :], scores, -jnp.inf)
    row_max = jnp.max(scores, axis=4)
    weights = jnp.exp(scores - row_max[..., None])
    row_total = jnp.sum(weights, axis=4)
    weighted = jnp.einsum(
        "trkgs,rskd->trkgd", weights, cache_values.astype(jnp.float32), precision=HIGHEST
    )
    return (weighted, row_max, row_total)


def recent_part(grouped, fresh_kv, score_scale):
    step_count = grouped.shape[0]
    scores = (
        jnp.einsum(
            "trkgd,urkd->trkgu", grouped, fresh_kv[:, :, 0], preferred_element_type=jnp.float32
        )
        * score_scale
    )
    causal = jnp.arange(step_count)[None, :] <= jnp.arange(step_count)[:, None]
    scores = jnp.where(causal[:, None, None, None, :], scores, -jnp.inf)
    row_max = jnp.max(scores, axis=4)
    weights = jnp.exp(scores - row_max[..., None])
    row_total = jnp.sum(weights, axis=4)
    weighted = jnp.einsum(
        "trkgu,urkd->trkgd", weights, fresh_kv[:, :, 1].astype(jnp.float32), precision=HIGHEST
    )
    return (weighted, row_max, row_total)


def mamba_steps(
    start_state,
    conv_rows,
    mamba_x,
    mamba_z,
    conv_weight,
    conv_bias,
    x_proj,
    dt_gain,
    dt_proj,
    dt_bias,
    a_log,
    skip_d,
):
    step_count = mamba_x.shape[0]
    tap_count = conv_weight.shape[0]
    rank_width = dt_proj.shape[0]
    state_size = a_log.shape[0]
    window = jnp.concatenate(
        [jnp.transpose(conv_rows, (1, 0, 2)), mamba_x.astype(jnp.float32)], axis=0
    )
    convolved = conv_bias + sum(
        (conv_weight[offset] * window[offset : offset + step_count] for offset in range(tap_count))
    )
    conv_out = jax.nn.silu(convolved).astype(jnp.bfloat16)
    inputs = conv_out.astype(jnp.float32)
    gate_values = jax.nn.silu(mamba_z.astype(jnp.float32))
    decay_log = -jnp.exp(a_log)
    hidden_state = start_state
    outputs = []
    for moment in range(step_count):
        current = lax.psum(
            jnp.dot(conv_out[moment], x_proj, preferred_element_type=jnp.float32), "tp"
        )
        dt_low = current[:, :rank_width]
        b_coef = current[:, rank_width : rank_width + state_size]
        c_coef = current[:, rank_width + state_size :]
        normed = (
            dt_low
            * lax.rsqrt(jnp.mean(dt_low * dt_low, axis=-1, keepdims=True) + EPSILON)
            * dt_gain
        ).astype(jnp.bfloat16)
        step_rate = jax.nn.softplus(
            jnp.dot(normed, dt_proj, preferred_element_type=jnp.float32) + dt_bias
        )
        hidden_state = (
            jnp.exp(step_rate[:, None, :] * decay_log[None]) * hidden_state
            + (step_rate * inputs[moment])[:, None, :] * b_coef[:, :, None]
        )
        reading = jnp.sum(c_coef[:, :, None] * hidden_state, axis=1) + skip_d * inputs[moment]
        outputs.append(reading * gate_values[moment])
    return jnp.stack(outputs).astype(jnp.bfloat16)


def per_device(
    queries,
    new_kv,
    prefill_page_pool,
    page_table,
    prompt_len,
    dest_device,
    ssm_state,
    conv_state,
    mamba_x,
    mamba_z,
    conv_weight,
    conv_bias,
    x_proj,
    dt_gain,
    dt_proj,
    dt_bias,
    a_log,
    skip_d,
):
    local_reqs = dest_device.shape[0]
    step_count = queries.shape[0]
    kv_heads = prefill_page_pool.shape[3] // HEAD_SIZE
    q_heads = queries.shape[2] // HEAD_SIZE
    group_width = q_heads // kv_heads
    cache_len = page_table.shape[1] * prefill_page_pool.shape[2]
    score_scale = 1.0 / math.sqrt(HEAD_SIZE)
    send_order = jnp.argsort(dest_device * local_reqs + jnp.arange(local_reqs, dtype=jnp.int32))
    grouped = queries.reshape(step_count, local_reqs, kv_heads, group_width, HEAD_SIZE)
    fresh_kv = new_kv.reshape(step_count, local_reqs, 2, kv_heads, HEAD_SIZE)
    picked = prefill_page_pool[page_table[send_order]]
    key_valid = jnp.arange(cache_len)[None, :] < prompt_len[send_order][:, None]
    arrived, arrived_mask = (
        lax.all_to_all(picked, "req", split_axis=0, concat_axis=0, tiled=True),
        lax.all_to_all(
            key_valid.astype(jnp.bfloat16), "req", split_axis=0, concat_axis=0, tiled=True
        ),
    )
    cache_keys = arrived[:, :, 0].reshape(local_reqs, cache_len, kv_heads, HEAD_SIZE)
    cache_values = arrived[:, :, 1].reshape(local_reqs, cache_len, kv_heads, HEAD_SIZE)
    weighted, row_max, row_total = cached_part(
        grouped, cache_keys, cache_values, arrived_mask > 0, score_scale
    )
    recent_weighted, recent_max, recent_total = recent_part(grouped, fresh_kv, score_scale)
    joint_max = jnp.maximum(row_max, recent_max)
    old_weight = jnp.exp(row_max - joint_max)
    new_weight = jnp.exp(recent_max - joint_max)
    combined = weighted * old_weight[..., None] + recent_weighted * new_weight[..., None]
    combined = combined / (row_total * old_weight + recent_total * new_weight)[..., None]
    attn_out = combined.reshape(step_count, local_reqs, q_heads * HEAD_SIZE).astype(jnp.bfloat16)
    moved_ssm, moved_conv = (
        lax.all_to_all(ssm_state[send_order], "req", split_axis=0, concat_axis=0, tiled=True),
        lax.all_to_all(
            conv_state[send_order].astype(jnp.float32),
            "req",
            split_axis=0,
            concat_axis=0,
            tiled=True,
        ),
    )
    mamba_out = mamba_steps(
        moved_ssm,
        moved_conv,
        mamba_x,
        mamba_z,
        conv_weight,
        conv_bias,
        x_proj,
        dt_gain,
        dt_proj,
        dt_bias,
        a_log,
        skip_d,
    )
    return (attn_out, mamba_out)


def solution(mesh):
    return jax.shard_map(
        per_device,
        mesh=mesh,
        in_specs=(
            P(None, "req", "tp"),
            P(None, "req", None, "tp"),
            P("req", None, None, "tp"),
            P("req", None),
            P("req"),
            P("req"),
            P("req", None, "tp"),
            P("req", None, "tp"),
            P(None, "req", "tp"),
            P(None, "req", "tp"),
            P(None, "tp"),
            P("tp"),
            P("tp", None),
            P(),
            P(None, "tp"),
            P("tp"),
            P(None, "tp"),
            P("tp"),
        ),
        out_specs=(P(None, "req", "tp"), P(None, "req", "tp")),
        check_vma=False,
    )
```

profile of v0, /device:TPU:0, one launch (start us, length us, event | category | flops | bytes accessed | tf_op | source)
XLA Modules:
  0.0 386.2 jit_solution(2727373946174895821)
XLA Ops:
  11.7 7.3 %all-to-all-start.1 = ((bf16[8,4,128]{2,1,0:T(4,128)(2,1)}), bf16[8,4,128]{2,1,0:T(4,128)(2,1)S(1)}, u32[]{:S(2)}, u32[]{:S(2)}) async-start(bf16[8,4,128]{2,1,0:T(4,128)(2,1)} %fusion.67), calls=%async_computation.1 | async-start | bytes 16384 | tf_op jit(solution)/shard_map/all_to_all | solution.py:137
  18.9 2.8 gather_fusion.3
  25.4 4.4 %all-to-all-start.2 = ((f32[32,3,4096]{2,1,0:T(4,128)}), f32[32,3,4096]{2,1,0:T(4,128)S(1)}, u32[]{:S(2)}, u32[]{:S(2)}) async-start(f32[32,3,4096]{2,1,0:T(4,128)} %copy.54), calls=%async_computation.2 | async-start | bytes 4194304 | tf_op jit(solution)/shard_map/all_to_all | solution.py:155
  30.6 5.0 %gather_fusion.1 = bf16[256,2,16,256]{3,2,1,0:T(8,128)(2,1)} fusion(bf16[256,2,16,256]{3,2,1,0:T(8,128)(2,1)} %param.20, s32[1024]{0:T(1024)S(1)} %pad_clamp_fusion), kind=kCustom, calls=%fused_computation.1 | custom fusion | bytes 8389632 | tf_op jit(solution)/shard_map/gather | solution.py:133
  35.6 4.8 %copy.45 = bf16[32,8,2,16,256]{4,3,1,2,0:T(8,128)(2,1)} copy(bf16[32,8,2,16,256]{4,3,2,1,0:T(8,128)(2,1)} %bitcast.116) | data formatting | bytes 8388608 | tf_op jit(solution)/shard_map/gather | solution.py:133
  40.3 37.2 %all-to-all-done.2 = f32[32,3,4096]{2,1,0:T(4,128)S(1)} async-done(((f32[32,3,4096]{2,1,0:T(4,128)}), f32[32,3,4096]{2,1,0:T(4,128)S(1)}, u32[]{:S(2)}, u32[]{:S(2)}) %all-to-all-start.2) | async-done | bytes 1572896 | tf_op jit(solution)/shard_map/all_to_all | solution.py:155
  77.5 4.5 %all-to-all-start = ((bf16[32,8,2,16,256]{4,3,1,2,0:T(8,128)(2,1)}), bf16[32,8,2,16,256]{4,3,1,2,0:T(8,128)(2,1)}, u32[]{:S(2)}, u32[]{:S(2)}) async-start(bf16[32,8,2,16,256]{4,3,1,2,0:T(8,128)(2,1)} %copy.45), calls=%async_computation | async-start | bytes 8388608 | tf_op jit(solution)/shard_map/all_to_all | solution.py:136
  82.0 7.7 %gather_fusion.4 = f32[32,16,4096]{2,1,0:T(8,128)} fusion(f32[32,16,4096]{2,1,0:T(8,128)} %param.24, s32[1024]{0:T(1024)S(1)} %pad_clamp_fusion.1), kind=kCustom, calls=%fused_computation.4 | custom fusion | bytes 16777344 | tf_op jit(solution)/shard_map/gather | solution.py:154
  89.7 84.9 %all-to-all-done = bf16[32,8,2,16,256]{4,3,1,2,0:T(8,128)(2,1)} async-done(((bf16[32,8,2,16,256]{4,3,1,2,0:T(8,128)(2,1)}), bf16[32,8,2,16,256]{4,3,1,2,0:T(8,128)(2,1)}, u32[]{:S(2)}, u32[]{:S(2)}) %all-to-all-start) | async-done | bytes 4194336 | tf_op jit(solution)/shard_map/all_to_all | solution.py:136
  174.6 5.0 %all-to-all-start.3 = ((f32[32,16,4096]{2,1,0:T(8,128)}), f32[32,16,4096]{2,1,0:T(8,128)}, u32[]{:S(2)}, u32[]{:S(2)}) async-start(f32[32,16,4096]{2,1,0:T(8,128)} %gather_fusion.4), calls=%async_computation.3 | async-start | bytes 16777216 | tf_op jit(solution)/shard_map/all_to_all | solution.py:154
  179.6 2.8 convert_element_type.44
  183.4 2.4 fusion.78
  188.8 3.6 convert_multiply_fusion
  202.8 34.0 %all-reduce.3.cloned.1.call-done = (f32[32,544]{1,0:T(8,128)}, f32[32,544]{1,0:T(8,128)}, f32[32,544]{1,0:T(8,128)}, f32[32,544]{1,0:T(8,128)}) async-done(((f32[32,544]{1,0:T(8,128)}, f32[32,544]{1,0:T(8,128)}, f32[32,544]{1,0:T(8,128)}, f32[32,544]{1,0:T(8,128)}), (f32[32,544]{1,0:T(8,128)}, f32[32,544]{1,0:T(8,128)}, f32[32,544]{1,0:T(8,128)}, f32[32,544]{1,0:T(8,128)})) %all-reduce.3.cloned.1.call-update) | async-done | bytes 278544 | tf_op jit(solution)/shard_map/psum | solution.py:80
  242.2 3.3 compare_select_fusion.3
  248.4 2.7 bitcast_multiply_fusion
  251.0 4.8 %fusion.71 = (bf16[32,8,1,16,256]{4,3,1,2,0:T(8,128)(2,1)}, bf16[32,8,1,16,256]{4,3,1,2,0:T(8,128)(2,1)}) fusion(bf16[32,8,2,16,256]{4,3,1,2,0:T(8,128)(2,1)} %all-to-all-done), kind=kLoop, calls=%fused_computation.129 | loop fusion | bytes 8388608 | tf_op jit(solution)/shard_map/slice | solution.py:142
  255.8 4.0 %reshape_squeeze.7 = bf16[32,128,2,128]{3,2,1,0:T(2,128)(2,1)} reshape(bf16[32,8,1,16,256]{4,3,1,2,0:T(8,128)(2,1)} %get-tuple-element.22) | data formatting | bytes 4194304 | tf_op jit(solution)/shard_map/reshape;squeeze | solution.py:141
  259.8 4.0 %reshape_squeeze.6 = bf16[32,128,2,128]{3,2,1,0:T(2,128)(2,1)} reshape(bf16[32,8,1,16,256]{4,3,1,2,0:T(8,128)(2,1)} %get-tuple-element.21) | data formatting | bytes 4194304 | tf_op jit(solution)/shard_map/reshape;squeeze | solution.py:142
  263.7 3.1 fusion.79
  269.0 2.3 fusion.40
  272.2 2.1 convert_element_type.42
  274.2 87.4 %all-to-all-done.3 = f32[32,16,4096]{2,1,0:T(8,128)} async-done(((f32[32,16,4096]{2,1,0:T(8,128)}), f32[32,16,4096]{2,1,0:T(8,128)}, u32[]{:S(2)}, u32[]{:S(2)}) %all-to-all-start.3) | async-done | bytes 8388640 | tf_op jit(solution)/shard_map/all_to_all | solution.py:154
  361.7 16.1 %multiply_reduce_fusion.1 = (f32[32,4096]{1,0:T(8,128)S(1)}, f32[32,4096]{1,0:T(8,128)S(1)}, f32[32,4096]{1,0:T(8,128)S(1)}, f32[32,4096]{1,0:T(8,128)S(1)}) fusion(f32[32,16]{1,0:T(8,128)S(1)} %copy-done.28, f32[32,4096]{1,0:T(8,128)} %get-tuple-element.24, f32[32,4096]{1,0:T(8,128)} %copy-done.5, f32[32,16]{1,0:T(8,128)S(1)} %copy-done.29, ...), kind=kLoop, calls=%fused_computation.6 | loop fusion | flops 49807360 | bytes 14958592 | tf_op jit(solution)/shard_map/reduce_sum | solution.py:98
  (114 shorter events, 35.9 us)
Async XLA Ops:
  7.2 11.8 %copy-start = (bf16[32,3,4096]{2,0,1:T(8,128)(2,1)S(1)}, bf16[32,3,4096]{2,0,1:T(8,128)(2,1)}, u32[]{:S(2)}) copy-start(bf16[32,3,4096]{2,0,1:T(8,128)(2,1)} %param.25) | copy-start | bytes 2359300
  11.7 13.8 %all-to-all-start.1 = ((bf16[8,4,128]{2,1,0:T(4,128)(2,1)}), bf16[8,4,128]{2,1,0:T(4,128)(2,1)S(1)}, u32[]{:S(2)}, u32[]{:S(2)}) async-start(bf16[8,4,128]{2,1,0:T(4,128)(2,1)} %fusion.67), calls=%async_computation.1 | async-start | bytes 16384 | tf_op jit(solution)/shard_map/all_to_all | solution.py:137
  25.4 52.1 %all-to-all-start.2 = ((f32[32,3,4096]{2,1,0:T(4,128)}), f32[32,3,4096]{2,1,0:T(4,128)S(1)}, u32[]{:S(2)}, u32[]{:S(2)}) async-start(f32[32,3,4096]{2,1,0:T(4,128)} %copy.54), calls=%async_computation.2 | async-start | bytes 4194304 | tf_op jit(solution)/shard_map/all_to_all | solution.py:155
  77.5 97.1 %all-to-all-start = ((bf16[32,8,2,16,256]{4,3,1,2,0:T(8,128)(2,1)}), bf16[32,8,2,16,256]{4,3,1,2,0:T(8,128)(2,1)}, u32[]{:S(2)}, u32[]{:S(2)}) async-start(bf16[32,8,2,16,256]{4,3,1,2,0:T(8,128)(2,1)} %copy.45), calls=%async_computation | async-start | bytes 8388608 | tf_op jit(solution)/shard_map/all_to_all | solution.py:136
  89.7 92.7 %copy-start.9 = (bf16[4,32,2048]{2,1,0:T(8,128)(2,1)S(1)}, bf16[4,32,2048]{2,1,0:T(8,128)(2,1)}, u32[]{:S(2)}) copy-start(bf16[4,32,2048]{2,1,0:T(8,128)(2,1)} %param.18) | copy-start | bytes 1572868
  174.6 187.0 %all-to-all-start.3 = ((f32[32,16,4096]{2,1,0:T(8,128)}), f32[32,16,4096]{2,1,0:T(8,128)}, u32[]{:S(2)}, u32[]{:S(2)}) async-start(f32[32,16,4096]{2,1,0:T(8,128)} %gather_fusion.4), calls=%async_computation.3 | async-start | bytes 16777216 | tf_op jit(solution)/shard_map/all_to_all | solution.py:154
  179.6 8.5 %copy-start.16 = (f32[16,4096]{1,0:T(8,128)S(1)}, f32[16,4096]{1,0:T(8,128)}, u32[]{:S(2)}) copy-start(f32[16,4096]{1,0:T(8,128)} %param.34) | copy-start | bytes 786436
  179.6 57.3 %all-reduce.3.cloned.1.call-start = ((), (), s32[]{:S(2)}) async-start(), calls=%async_computation.4 | async-start | bytes 655360 | tf_op jit(solution)/shard_map/psum | solution.py:80
  182.6 10.7 %copy-start.10 = (bf16[16,8,16,128]{3,2,1,0:T(8,128)(2,1)}, bf16[16,8,16,128]{3,2,1,0:T(8,128)(2,1)S(1)}, u32[]{:S(2)}) copy-start(bf16[16,8,16,128]{3,2,1,0:T(8,128)(2,1)S(1)} %copy.69) | copy-start | bytes 1572868
  185.9 8.7 %copy-start.7 = (f32[4,32,2,8,4]{3,4,0,2,1:T(4,128)}, f32[4,32,2,8,4]{3,4,0,2,1:T(4,128)S(1)}, u32[]{:S(2)}) copy-start(f32[4,32,2,8,4]{3,4,0,2,1:T(4,128)S(1)} %get-tuple-element.42) | copy-start | bytes 98308
  198.7 43.5 %copy-start.15 = (f32[4096]{0:T(1024)S(1)}, f32[4096]{0:T(1024)}, u32[]{:S(2)}) copy-start(f32[4096]{0:T(1024)} %param.33) | copy-start | bytes 49156
  198.7 43.5 %copy-start.19 = (f32[512]{0:T(512)S(1)}, f32[512]{0:T(512)}, u32[]{:S(2)}) copy-start(f32[512]{0:T(512)} %param.31) | copy-start | bytes 6148
  236.9 8.6 %copy-start.2 = (bf16[512,4096]{1,0:T(8,128)(2,1)S(1)}, bf16[512,4096]{1,0:T(8,128)(2,1)}, u32[]{:S(2)}) copy-start(bf16[512,4096]{1,0:T(8,128)(2,1)} %param.32) | copy-start | bytes 12582916
  236.9 8.6 %copy-start.14 = (f32[32,544]{1,0:T(8,128)S(1)}, f32[32,544]{1,0:T(8,128)}, u32[]{:S(2)}) copy-start(f32[32,544]{1,0:T(8,128)} %get-tuple-element.9) | copy-start | bytes 208900
  268.9 92.7 %copy-start.22 = (f32[32,16]{1,0:T(8,128)S(1)}, f32[32,16]{1,0:T(8,128)}, u32[]{:S(2)}) copy-start(f32[32,16]{1,0:T(8,128)} %get-tuple-element.29) | copy-start | bytes 6148
  268.9 92.6 %copy-start.23 = (f32[32,16]{1,0:T(8,128)S(1)}, f32[32,16]{1,0:T(8,128)}, u32[]{:S(2)}) copy-start(f32[32,16]{1,0:T(8,128)} %get-tuple-element.30) | copy-start | bytes 6148
  268.9 92.6 %copy-start.24 = (f32[32,16]{1,0:T(8,128)S(1)}, f32[32,16]{1,0:T(8,128)}, u32[]{:S(2)}) copy-start(f32[32,16]{1,0:T(8,128)} %get-tuple-element.50) | copy-start | bytes 6148
  269.0 92.6 %copy-start.25 = (f32[32,16]{1,0:T(8,128)S(1)}, f32[32,16]{1,0:T(8,128)}, u32[]{:S(2)}) copy-start(f32[32,16]{1,0:T(8,128)} %get-tuple-element.51) | copy-start | bytes 6148
  269.0 92.6 %copy-start.26 = (f32[32,16]{1,0:T(8,128)S(1)}, f32[32,16]{1,0:T(8,128)}, u32[]{:S(2)}) copy-start(f32[32,16]{1,0:T(8,128)} %get-tuple-element.33) | copy-start | bytes 6148
  269.0 92.6 %copy-start.27 = (f32[32,16]{1,0:T(8,128)S(1)}, f32[32,16]{1,0:T(8,128)}, u32[]{:S(2)}) copy-start(f32[32,16]{1,0:T(8,128)} %get-tuple-element.34) | copy-start | bytes 6148
  269.0 92.6 %copy-start.28 = (f32[32,16]{1,0:T(8,128)S(1)}, f32[32,16]{1,0:T(8,128)}, u32[]{:S(2)}) copy-start(f32[32,16]{1,0:T(8,128)} %get-tuple-element.52) | copy-start | bytes 6148
  269.0 92.6 %copy-start.29 = (f32[32,16]{1,0:T(8,128)S(1)}, f32[32,16]{1,0:T(8,128)}, u32[]{:S(2)}) copy-start(f32[32,16]{1,0:T(8,128)} %get-tuple-element.53) | copy-start | bytes 6148
  361.6 16.1 %copy-start.3 = (f32[4,32,4096]{2,1,0:T(8,128)S(1)}, f32[4,32,4096]{2,1,0:T(8,128)}, u32[]{:S(2)}) copy-start(f32[4,32,4096]{2,1,0:T(8,128)} %convert_multiply_fusion) | copy-start | bytes 6291460
  361.6 16.1 %copy-start.21 = (f32[4096]{0:T(1024)S(1)}, f32[4096]{0:T(1024)}, u32[]{:S(2)}) copy-start(f32[4096]{0:T(1024)} %param.35) | copy-start | bytes 49156
  (14 other events, 58.2 us)
Sparse Core Ops, SparseCore 0:
  202.9 33.8 all-reduce.2
where the time goes:
time: 387 us; the launch traced here: 386 us
  waiting for transfers between devices  245 us (63%)
  local copies, waits for them, and re-layouts  46.9 us (12%)
  other arithmetic  33.4 us (9%)
  matrix products  25.1 us (6%)
  starting transfers between devices  21.2 us (5%)
  between operations  14.6 us (4%)
    all_to_all x1, waiting for transfers between devices, per_device(): lax.all_to_all(ssm_state[send_order], 'req', split_axis=0, concat_axis=0,...  87.4 us
    all_to_all x1, waiting for transfers between devices, per_device(): lax.all_to_all(picked, 'req', split_axis=0, concat_axis=0, tiled=True)  84.9 us
    all_to_all x1, waiting for transfers between devices, per_device(): lax.all_to_all(conv_state[send_order].astype(jnp.float32), 'req', split_a...  37.2 us
    psum x1, waiting for transfers between devices, mamba_steps(): lax.psum(jnp.dot(conv_out[moment], x_proj, preferred_element_type=jnp.flo...  34 us
    reduce_sum x1, other arithmetic, mamba_steps(): jnp.sum(c_coef[:, :, None] * hidden_state, axis=1) + skip_d * inputs[moment]  16.1 us
    gather x3, local copies, waits for them, and re-layouts, per_device(): picked = prefill_page_pool[page_table[send_order]]  10.3 us
    dot_general x4, matrix products, mamba_steps(): jnp.dot(conv_out[moment], x_proj, preferred_element_type=jnp.float32)  8.14 us
    dot_general x4, matrix products, mamba_steps(): jnp.dot(normed, dt_proj, preferred_element_type=jnp.float32) + dt_bias  7.95 us
  transfers between devices with their start and end apart: 5, of which 5 were waited for; matrix products, arithmetic and copies ran while one was open for 21% of the time, Pallas kernels for 0%

commit v1 on v0

v1 whole, which is shorter than its diff:
```python
import math

import jax
import jax.numpy as jnp
from jax import lax
from jax.sharding import PartitionSpec as P

HEAD_SIZE = 128


EPSILON = 1e-06
HIGHEST = lax.Precision.HIGHEST


def cached_part(grouped, cache_keys, cache_values, key_valid, score_scale):
    scores = (
        jnp.einsum("trkgd,rskd->trkgs", grouped, cache_keys, preferred_element_type=jnp.float32)
        * score_scale
    )
    scores = jnp.where(key_valid[None, :, None, None, :], scores, -jnp.inf)
    row_max = jnp.max(scores, axis=4)
    weights = jnp.exp(scores - row_max[..., None])
    row_total = jnp.sum(weights, axis=4)
    weighted = jnp.einsum(
        "trkgs,rskd->trkgd", weights, cache_values.astype(jnp.float32), precision=HIGHEST
    )
    return (weighted, row_max, row_total)


def recent_part(grouped, fresh_kv, score_scale):
    step_count = grouped.shape[0]
    scores = (
        jnp.einsum(
            "trkgd,urkd->trkgu", grouped, fresh_kv[:, :, 0], preferred_element_type=jnp.float32
        )
        * score_scale
    )
    causal = jnp.arange(step_count)[None, :] <= jnp.arange(step_count)[:, None]
    scores = jnp.where(causal[:, None, None, None, :], scores, -jnp.inf)
    row_max = jnp.max(scores, axis=4)
    weights = jnp.exp(scores - row_max[..., None])
    row_total = jnp.sum(weights, axis=4)
    weighted = jnp.einsum(
        "trkgu,urkd->trkgd", weights, fresh_kv[:, :, 1].astype(jnp.float32), precision=HIGHEST
    )
    return (weighted, row_max, row_total)


def sum_over_tp(value):
    width = lax.axis_size("tp")
    hop = 1
    while hop < width:
        pairs = [(index, index ^ hop) for index in range(width)]
        value = value + lax.ppermute(value, "tp", pairs)
        hop *= 2
    return value


def swap_rows(value):
    return lax.all_to_all(value, "req", split_axis=1, concat_axis=1, tiled=True)


def mamba_readings(
    start_state, conv_rows, rows_x, conv_weight, conv_bias, x_proj, dt_gain, dt_proj, dt_bias, a_log, skip_d
):
    step_count = rows_x.shape[0]
    tap_count = conv_weight.shape[0]
    rank_width = dt_proj.shape[0]
    state_size = a_log.shape[0]
    window = jnp.concatenate([jnp.transpose(conv_rows, (1, 0, 2)), rows_x], axis=0).astype(jnp.float32)
    convolved = conv_bias + sum(
        (conv_weight[offset] * window[offset : offset + step_count] for offset in range(tap_count))
    )
    conv_out = jax.nn.silu(convolved).astype(jnp.bfloat16)
    inputs = conv_out.astype(jnp.float32)
    decay_log = -jnp.exp(a_log)
    proj = sum_over_tp(
        jnp.einsum("trc,cw->trw", conv_out, x_proj, preferred_element_type=jnp.float32)
    )
    dt_low = proj[..., :rank_width]
    b_coef = proj[..., rank_width : rank_width + state_size]
    c_coef = proj[..., rank_width + state_size :]
    normed = (
        dt_low
        * lax.rsqrt(jnp.mean(dt_low * dt_low, axis=-1, keepdims=True) + EPSILON)
        * dt_gain
    ).astype(jnp.bfloat16)
    step_rate = jax.nn.softplus(
        jnp.einsum("trk,kc->trc", normed, dt_proj, preferred_element_type=jnp.float32) + dt_bias
    )
    hidden_state = start_state
    outputs = []
    for moment in range(step_count):
        rate = step_rate[moment]
        hidden_state = (
            jnp.exp(rate[:, None, :] * decay_log[None]) * hidden_state
            + (rate * inputs[moment])[:, None, :] * b_coef[moment][:, :, None]
        )
        reading = jnp.sum(c_coef[moment][:, :, None] * hidden_state, axis=1) + skip_d * inputs[moment]
        outputs.append(reading)
    return jnp.stack(outputs)


def per_device(
    queries,
    new_kv,
    prefill_page_pool,
    page_table,
    prompt_len,
    dest_device,
    ssm_state,
    conv_state,
    mamba_x,
    mamba_z,
    conv_weight,
    conv_bias,
    x_proj,
    dt_gain,
    dt_proj,
    dt_bias,
    a_log,
    skip_d,
):
    local_reqs = dest_device.shape[0]
    step_count = queries.shape[0]
    kv_heads = prefill_page_pool.shape[3] // HEAD_SIZE
    q_heads = queries.shape[2] // HEAD_SIZE
    group_width = q_heads // kv_heads
    cache_len = page_table.shape[1] * prefill_page_pool.shape[2]
    score_scale = 1.0 / math.sqrt(HEAD_SIZE)
    share = local_reqs // lax.axis_size("req")
    index = jnp.arange(local_reqs, dtype=jnp.int32)
    same = dest_device[:, None] == dest_device[None, :]
    rank = jnp.sum((same & (index[None, :] < index[:, None])).astype(jnp.int32), axis=1)
    slot = dest_device * share + rank
    to_home = (slot[:, None] == index[None, :]).astype(jnp.bfloat16)
    moved_x = swap_rows(mamba_x)
    moved_q = swap_rows(queries)
    moved_kv = swap_rows(new_kv.reshape(step_count, local_reqs, -1))
    rows_x = jnp.einsum("ks,tsc->tkc", to_home, moved_x)
    rows_q = jnp.einsum("ks,tsc->tkc", to_home, moved_q)
    rows_kv = jnp.einsum("ks,tsc->tkc", to_home, moved_kv)
    readings = mamba_readings(
        ssm_state, conv_state, rows_x, conv_weight, conv_bias, x_proj, dt_gain, dt_proj, dt_bias, a_log, skip_d
    ).astype(jnp.bfloat16)
    back_y = swap_rows(jnp.einsum("ks,tkc->tsc", to_home, readings))
    grouped = rows_q.reshape(step_count, local_reqs, kv_heads, group_width, HEAD_SIZE)
    fresh_kv = rows_kv.reshape(step_count, local_reqs, 2, kv_heads, HEAD_SIZE)
    picked = prefill_page_pool[page_table]
    key_valid = jnp.arange(cache_len)[None, :] < prompt_len[:, None]
    cache_keys = picked[:, :, 0].reshape(local_reqs, cache_len, kv_heads, HEAD_SIZE)
    cache_values = picked[:, :, 1].reshape(local_reqs, cache_len, kv_heads, HEAD_SIZE)
    weighted, row_max, row_total = cached_part(
        grouped, cache_keys, cache_values, key_valid, score_scale
    )
    recent_weighted, recent_max, recent_total = recent_part(grouped, fresh_kv, score_scale)
    joint_max = jnp.maximum(row_max, recent_max)
    old_weight = jnp.exp(row_max - joint_max)
    new_weight = jnp.exp(recent_max - joint_max)
    combined = weighted * old_weight[..., None] + recent_weighted * new_weight[..., None]
    combined = combined / (row_total * old_weight + recent_total * new_weight)[..., None]
    rows_out = combined.reshape(step_count, local_reqs, q_heads * HEAD_SIZE).astype(jnp.bfloat16)
    attn_out = swap_rows(jnp.einsum("ks,tkc->tsc", to_home, rows_out))
    gate_values = jax.nn.silu(mamba_z.astype(jnp.float32))
    mamba_out = (back_y.astype(jnp.float32) * gate_values).astype(jnp.bfloat16)
    return (attn_out, mamba_out)


def solution(mesh):
    return jax.shard_map(
        per_device,
        mesh=mesh,
        in_specs=(
            P(None, "req", "tp"),
            P(None, "req", None, "tp"),
            P("req", None, None, "tp"),
            P("req", None),
            P("req"),
            P("req"),
            P("req", None, "tp"),
            P("req", None, "tp"),
            P(None, "req", "tp"),
            P(None, "req", "tp"),
            P(None, "tp"),
            P("tp"),
            P("tp", None),
            P(),
            P(None, "tp"),
            P("tp"),
            P(None, "tp"),
            P("tp"),
        ),
        out_specs=(P(None, "req", "tp"), P(None, "req", "tp")),
        check_vma=False,
    )
```

time: 387 us -> 148 us (0.38)
  waiting for transfers between devices: 245 us -> 46.2 us
  local copies, waits for them, and re-layouts: 46.9 us -> 32.5 us
  between operations: 14.6 us -> 1.06 us
  other arithmetic: 33.4 us -> 22.3 us
  matrix products: 25.1 us -> 17.5 us
  starting transfers between devices: 21.2 us -> 27.6 us
    all_to_all x4 -> x5, waiting for transfers between devices: 211 us -> 45.4 us  [swap_rows(): return lax.all_to_all(value, 'req', split_axis=1, concat_axis=1, tiled=True)]
    psum x1 -> x0, waiting for transfers between devices: 34 us -> none  [mamba_steps(): lax.psum(jnp.dot(conv_out[moment], x_proj, preferred_element_type=jnp.flo...]
    gather x6 -> x1, local copies, waits for them, and re-layouts: 22.2 us -> 4.95 us  [per_device(): picked = prefill_page_pool[page_table]]
    unnamed x68 -> x65, local copies, waits for them, and re-layouts: 1.13 us -> 13.6 us
    slice x4 -> x1, local copies, waits for them, and re-layouts: 8.78 us -> 1.67 us  [mamba_readings(): conv_weight[offset] * window[offset:offset + step_count]]
    dot_general x8 -> x7, matrix products: 16.1 us -> 10.2 us  [the longest x1 4.11 us: mamba_readings(): jnp.einsum('trk,kc->trc', normed, dt_proj, preferred_element_type=jnp.flo...]
    all_to_all x4 -> x5, starting transfers between devices: 21.1 us -> 26 us  [swap_rows(): return lax.all_to_all(value, 'req', split_axis=1, concat_axis=1, tiled=True)]
    reduce_sum x3, other arithmetic: 18.4 us -> 14.3 us  [the longest x1 14 us: mamba_readings(): jnp.sum(c_coef[moment][:, :, None] * hidden_state, axis=1)]
  transfers between devices with their start and end apart: 5 -> 7, of which waited for: 5 -> 5; matrix products, arithmetic and copies ran while one was open for 21% -> 41% of each run, Pallas kernels for 0% -> 0%
where the time goes in v1:
time: 148 us; the launch traced here: 147 us
  waiting for transfers between devices  46.2 us (31%)
  local copies, waits for them, and re-layouts  32.5 us (22%)
  starting transfers between devices  27.6 us (19%)
  other arithmetic  22.3 us (15%)
  matrix products  17.5 us (12%)
    all_to_all x5, waiting for transfers between devices, swap_rows(): return lax.all_to_all(value, 'req', split_axis=1, concat_axis=1, tiled=True)  45.4 us
    all_to_all x5, starting transfers between devices, swap_rows(): return lax.all_to_all(value, 'req', split_axis=1, concat_axis=1, tiled=True)  26 us
    reduce_sum x1, other arithmetic, mamba_readings(): jnp.sum(c_coef[moment][:, :, None] * hidden_state, axis=1)  14 us
    unnamed x65, local copies, waits for them, and re-layouts  13.6 us
    gather x1, local copies, waits for them, and re-layouts, per_device(): picked = prefill_page_pool[page_table]  4.95 us
    dot_general x1, matrix products, mamba_readings(): jnp.einsum('trk,kc->trc', normed, dt_proj, preferred_element_type=jnp.flo...  4.11 us
    another operation x1, local copies, waits for them, and re-layouts, per_device(): picked[:, :, 0].reshape(local_reqs, cache_len, kv_heads, HEAD_SIZE)  3.96 us
  transfers between devices with their start and end apart: 7, of which 5 were waited for; matrix products, arithmetic and copies ran while one was open for 41% of the time, Pallas kernels for 0%

profile of v1, /device:TPU:0, one launch (start us, length us, event | category | flops | bytes accessed | tf_op | source)
XLA Modules:
  0.0 147.2 jit_solution(4004290690848515540)
XLA Ops:
  2.4 7.3 %all-to-all-start.1 = ((bf16[4,32,512]{2,0,1:T(4,128)(2,1)}), bf16[4,32,512]{2,0,1:T(4,128)(2,1)S(1)}, u32[]{:S(2)}, u32[]{:S(2)}) async-start(bf16[4,32,512]{2,0,1:T(4,128)(2,1)} %copy.99), calls=%async_computation.1 | async-start | bytes 262144 | tf_op jit(solution)/shard_map/all_to_all | solution.py:60
  10.5 1.7 %fusion.87 = (f32[1,4096]{1,0:T(1,128)S(1)}, f32[1,4096]{1,0:T(1,128)}, f32[1,4096]{1,0:T(1,128)}, f32[1,4096]{1,0:T(1,128)}) fusion(f32[4,4096]{1,0:T(4,128)} %param.28), kind=kLoop, calls=%fused_computation.127 | loop fusion | bytes 131072 | tf_op jit(solution)/shard_map/slice | solution.py:72
  12.2 5.0 %gather_fusion = bf16[256,2,16,256]{3,2,1,0:T(8,128)(2,1)} fusion(bf16[256,2,16,256]{3,2,1,0:T(8,128)(2,1)} %param.20, s32[1024]{0:T(1024)S(1)} %pad_clamp_fusion), kind=kCustom, calls=%fused_computation | custom fusion | bytes 8389632 | tf_op jit(solution)/shard_map/gather | solution.py:149
  17.1 4.1 %slice_bitcast_fusion.1 = (bf16[32,8,1,16,256]{4,3,1,0,2:T(8,128)(2,1)S(1)}, bf16[32,8,1,16,256]{4,3,1,0,2:T(8,128)(2,1)}) fusion(bf16[32,8,2,16,256]{4,3,2,1,0:T(8,128)(2,1)} %bitcast.152), kind=kLoop, calls=%fused_computation.31 | loop fusion | bytes 8388608
  22.5 6.0 %all-to-all-start = ((bf16[4,32,2048]{2,0,1:T(4,128)(2,1)}), bf16[4,32,2048]{2,0,1:T(4,128)(2,1)S(1)}, u32[]{:S(2)}, u32[]{:S(2)}) async-start(bf16[4,32,2048]{2,0,1:T(4,128)(2,1)} %copy.66), calls=%async_computation | async-start | bytes 1048576 | tf_op jit(solution)/shard_map/all_to_all | solution.py:60
  28.7 3.0 %copy.80 = bf16[4,32,4096]{2,0,1:T(4,128)(2,1)} copy(bf16[4,32,4096]{2,1,0:T(8,128)(2,1)} %param.26) | data formatting | bytes 2097152 | tf_op args[8]
  32.4 10.0 %all-to-all-done = bf16[4,32,2048]{2,0,1:T(4,128)(2,1)S(1)} async-done(((bf16[4,32,2048]{2,0,1:T(4,128)(2,1)}), bf16[4,32,2048]{2,0,1:T(4,128)(2,1)S(1)}, u32[]{:S(2)}, u32[]{:S(2)}) %all-to-all-start) | async-done | bytes 524320 | tf_op jit(solution)/shard_map/all_to_all | solution.py:60
  43.3 3.7 %all-to-all-start.3 = ((bf16[4,32,4096]{2,0,1:T(4,128)(2,1)}), bf16[4,32,4096]{2,0,1:T(4,128)(2,1)S(1)}, u32[]{:S(2)}, u32[]{:S(2)}) async-start(bf16[4,32,4096]{2,0,1:T(4,128)(2,1)} %copy.80), calls=%async_computation.3 | async-start | bytes 2097152 | tf_op jit(solution)/shard_map/all_to_all | solution.py:60
  47.0 4.0 %reshape_squeeze.7 = bf16[32,128,2,128]{3,2,1,0:T(2,128)(2,1)} reshape(bf16[32,8,1,16,256]{4,3,1,0,2:T(8,128)(2,1)} %get-tuple-element.20) | data formatting | bytes 4194304 | tf_op jit(solution)/shard_map/reshape;squeeze | solution.py:151
  51.0 2.0 %reshape_squeeze.6 = bf16[32,128,2,128]{3,2,1,0:T(2,128)(2,1)} reshape(bf16[32,8,1,16,256]{4,3,1,0,2:T(8,128)(2,1)S(1)} %get-tuple-element.19) | data formatting | bytes 4194304 | tf_op jit(solution)/shard_map/reshape;squeeze | solution.py:152
  54.1 1.9 %fusion.58 = bf16[32,4,2048]{2,0,1:T(8,128)(2,1)S(1)} fusion(bf16[4,32,2048]{2,0,1:T(4,128)(2,1)} %copy-done.2, s32[32]{0:T(128)S(1)} %multiply_add_fusion.4), kind=kOutput, calls=%fused_computation.79 | convolution fusion | flops 16778240 | bytes 1048704 | tf_op jit(solution)/shard_map/ks,tsc->tkc/dot_general | solution.py:141
  56.1 2.4 %fusion.88 = (f32[4,32,2,8]{3,0,2,1:T(4,128)S(1)}, f32[4,32,2,8,4]{3,4,0,2,1:T(4,128)S(1)}) fusion(bf16[4,32,2,8,128]{4,3,2,1,0:T(8,128)(2,1)S(1)} %bitcast.161, bf16[4,32,1,2,128]{4,3,2,1,0:T(2,128)(2,1)S(1)} %get-tuple-element.38, pred[4,4]{1,0:T(4,128)(4,1)S(1)} %iota_compare_fusion.3), kind=kOutput, calls=%fused_computation.128 | convolution fusion | flops 2119680 | bytes 630800 | tf_op jit(solution)/shard_map/trkgd,urkd->trkgu/dot_general | solution.py:33
  61.8 10.7 %all-to-all-done.3 = bf16[4,32,4096]{2,0,1:T(4,128)(2,1)S(1)} async-done(((bf16[4,32,4096]{2,0,1:T(4,128)(2,1)}), bf16[4,32,4096]{2,0,1:T(4,128)(2,1)S(1)}, u32[]{:S(2)}, u32[]{:S(2)}) %all-to-all-start.3) | async-done | bytes 1048608 | tf_op jit(solution)/shard_map/all_to_all | solution.py:60
  76.5 1.7 %fusion = f32[4,32,544]{2,1,0:T(8,128)S(1)} fusion(bf16[4,32,4096]{2,1,0:T(8,128)(2,1)S(1)} %get-tuple-element.11, bf16[4096,544]{0,1:T(8,128)(2,1)S(1)} %bitcast.154), kind=kOutput, calls=%fused_computation.12 | convolution fusion | flops 570425344 | bytes 5783552 | tf_op jit(solution)/shard_map/trc,cw->trw/dot_general | solution.py:78
  80.0 1.6 %collective-permute-start.1 = (f32[4,32,544]{2,1,0:T(8,128)S(1)}, f32[4,32,544]{2,1,0:T(8,128)}, u32[]{:S(2)}, u32[]{:S(2)}) collective-permute-start(f32[4,32,544]{2,1,0:T(8,128)S(1)} %add.111), channel_id=1, source_target_pairs={{0,2},{1,3},{2,0},{3,1},{4,6},{5,7},{6,4},{7,5},{8,10},{9,11},{10,... | collective-permute-start | bytes 835592 | tf_op jit(solution)/shard_map/ppermute | solution.py:54
  81.5 2.2 %fusion.42 = bf16[4,32,2,8,128]{4,3,0,2,1:T(8,128)(2,1)S(1)} fusion(f32[4,32,2,8,128]{4,3,0,2,1:T(8,128)S(1)} %fusion.27, bf16[32,128,2,128,1]{3,2,1,0,4:T(2,128)(2,1)S(1)} %bitcast.155, f32[4,32,2,8,128]{4,3,0,2,1:T(8,128)S(1)} %get-tuple-element.46, f32[4,32,2,8]{3,0,2,1:T(4,128)S(1)} %bitcast.165, f32[4,32,2,8]{3,0,2,1:T(4,128)S(1)} %bitcast.166, ...), kind=kOutput, calls=%fused_computation.51 | convolution fusion | flops 403963904 | bytes 4743168 | tf_op jit(solution)/shard_map/trkgs,rskd->trkgd/dot_general | solution.py:24
  85.9 3.5 %all-to-all-start.2 = ((bf16[4,32,2048]{2,0,1:T(4,128)(2,1)}), bf16[4,32,2048]{2,0,1:T(4,128)(2,1)S(1)}, u32[]{:S(2)}, u32[]{:S(2)}) async-start(bf16[4,32,2048]{2,0,1:T(4,128)(2,1)} %copy.79), calls=%async_computation.2 | async-start | bytes 1048576 | tf_op jit(solution)/shard_map/all_to_all | solution.py:60
  91.3 4.1 %compare_select_fusion = f32[4,32,4096]{2,1,0:T(8,128)S(1)} fusion(bf16[512,4096]{1,0:T(8,128)(2,1)} %param.32, f32[4096]{0:T(1024)S(1)} %copy-done.23, f32[4,32,544]{2,1,0:T(8,128)S(1)} %add.112, f32[512]{0:T(512)S(1)} %copy-done.24, f32[4,32]{1,0:T(4,128)S(1)} %add_rsqrt_fusion), kind=kOutput, calls=%fused_computation.8 | convolution fusion | flops 540737536 | bytes 6574080 | tf_op jit(solution)/shard_map/trk,kc->trc/dot_general | solution.py:89
  95.9 1.7 %slice-done.3 = s8[4194304]{0:T(1024)(128)(4,1)S(1)} async-done(((s8[8388608]{0:T(1024)(128)(4,1)}), s8[4194304]{0:T(1024)(128)(4,1)S(1)}, s32[]{:S(2)}) %slice-start.3) | async-done | bytes 4194328
  97.6 14.0 %multiply_reduce_fusion.1 = (f32[32,4096]{1,0:T(8,128)S(1)}, f32[32,4096]{1,0:T(8,128)S(1)}, f32[32,4096]{1,0:T(8,128)S(1)}, f32[32,4096]{1,0:T(8,128)S(1)}) fusion(f32[32,16]{1,0:T(8,128)S(1)} %get-tuple-element.32, f32[32,4096]{1,0:T(8,128)S(1)} %get-tuple-element.16, f32[32,4096]{1,0:T(8,128)S(1)} %get-tuple-element.26, ...), kind=kLoop, calls=%fused_computation.2 | loop fusion | flops 49807360 | bytes 14958592 | tf_op jit(solution)/shard_map/reduce_sum | solution.py:99
  112.4 1.8 %copy.83 = bf16[4,32,4096]{2,0,1:T(4,128)(2,1)} copy(bf16[4,32,4096]{2,1,0:T(8,128)(2,1)S(1)} %convolution_bitcast_fusion) | data formatting | bytes 2097152 | tf_op jit(solution)/shard_map/ks,tkc->tsc/transpose | solution.py:146
  114.2 5.5 %all-to-all-start.4 = ((bf16[4,32,4096]{2,0,1:T(4,128)(2,1)}), bf16[4,32,4096]{2,0,1:T(4,128)(2,1)S(1)}, u32[]{:S(2)}, u32[]{:S(2)}) async-start(bf16[4,32,4096]{2,0,1:T(4,128)(2,1)} %copy.83), calls=%async_computation.4 | async-start | bytes 2097152 | tf_op jit(solution)/shard_map/all_to_all | solution.py:60
  120.7 24.6 %all-to-all-done.4 = bf16[4,32,4096]{2,0,1:T(4,128)(2,1)S(1)} async-done(((bf16[4,32,4096]{2,0,1:T(4,128)(2,1)}), bf16[4,32,4096]{2,0,1:T(4,128)(2,1)S(1)}, u32[]{:S(2)}, u32[]{:S(2)}) %all-to-all-start.4) | async-done | bytes 1048608 | tf_op jit(solution)/shard_map/all_to_all | solution.py:60
  145.3 1.8 %fusion.17 = bf16[4,32,4096]{2,1,0:T(8,128)(2,1)} fusion(bf16[4,32,4096]{2,1,0:T(8,128)(2,1)S(1)} %copy-done.3, bf16[4,32,4096]{2,0,1:T(4,128)(2,1)S(1)} %all-to-all-done.4), kind=kLoop, calls=%fused_computation.37 | loop fusion | flops 4194304 | bytes 3145728 | tf_op jit(solution)/shard_map/convert_element_type | solution.py:165
  (104 shorter events, 21.7 us)
Async XLA Ops:
  2.4 20.1 %all-to-all-start.1 = ((bf16[4,32,512]{2,0,1:T(4,128)(2,1)}), bf16[4,32,512]{2,0,1:T(4,128)(2,1)S(1)}, u32[]{:S(2)}, u32[]{:S(2)}) async-start(bf16[4,32,512]{2,0,1:T(4,128)(2,1)} %copy.99), calls=%async_computation.1 | async-start | bytes 262144 | tf_op jit(solution)/shard_map/all_to_all | solution.py:60
  17.1 4.1 %copy-start.9 = (bf16[4,32,2048]{2,1,0:T(8,128)(2,1)S(1)}, bf16[4,32,2048]{2,1,0:T(8,128)(2,1)}, u32[]{:S(2)}) copy-start(bf16[4,32,2048]{2,1,0:T(8,128)(2,1)} %param.18) | copy-start | bytes 1572868
  17.1 5.3 %copy-start.22 = (s32[32]{0:T(128)S(1)}, s32[32]{0:T(128)}, u32[]{:S(2)}) copy-start(s32[32]{0:T(128)} %param.22) | copy-start | bytes 388
  21.2 7.3 %copy-start.25 = (s32[32]{0:T(128)S(1)}, s32[32]{0:T(128)}, u32[]{:S(2)}) copy-start(s32[32]{0:T(128)} %param.23) | copy-start | bytes 388
  21.2 10.5 %copy-start.11 = (f32[16,4096]{1,0:T(8,128)S(1)}, f32[16,4096]{1,0:T(8,128)}, u32[]{:S(2)}) copy-start(f32[16,4096]{1,0:T(8,128)} %param.34) | copy-start | bytes 786436
  22.5 20.0 %all-to-all-start = ((bf16[4,32,2048]{2,0,1:T(4,128)(2,1)}), bf16[4,32,2048]{2,0,1:T(4,128)(2,1)S(1)}, u32[]{:S(2)}, u32[]{:S(2)}) async-start(bf16[4,32,2048]{2,0,1:T(4,128)(2,1)} %copy.66), calls=%async_computation | async-start | bytes 1048576 | tf_op jit(solution)/shard_map/all_to_all | solution.py:60
  43.3 29.3 %all-to-all-start.3 = ((bf16[4,32,4096]{2,0,1:T(4,128)(2,1)}), bf16[4,32,4096]{2,0,1:T(4,128)(2,1)S(1)}, u32[]{:S(2)}, u32[]{:S(2)}) async-start(bf16[4,32,4096]{2,0,1:T(4,128)(2,1)} %copy.80), calls=%async_computation.3 | async-start | bytes 2097152 | tf_op jit(solution)/shard_map/all_to_all | solution.py:60
  47.0 7.0 %copy-start.19 = (s32[32]{0:T(128)}, s32[32]{0:T(128)S(1)}, u32[]{:S(2)}) copy-start(s32[32]{0:T(128)S(1)} %multiply_add_fusion.4) | copy-start | bytes 388
  54.1 5.6 %copy-start.1 = (bf16[32,128,2,128]{3,2,1,0:T(2,128)(2,1)S(1)}, bf16[32,128,2,128]{3,2,1,0:T(2,128)(2,1)}, u32[]{:S(2)}) copy-start(bf16[32,128,2,128]{3,2,1,0:T(2,128)(2,1)} %reshape_squeeze.7) | copy-start | bytes 6291460
  59.7 12.9 %copy-start.20 = (s32[32]{0:T(128)S(1)}, s32[32]{0:T(128)}, u32[]{:S(2)}) copy-start(s32[32]{0:T(128)} %copy-done.19) | copy-start | bytes 388
  61.0 17.3 %copy-start.5 = (f32[4,32,2,8]{3,0,2,1:T(4,128)}, f32[4,32,2,8]{3,0,2,1:T(4,128)S(1)}, u32[]{:S(2)}) copy-start(f32[4,32,2,8]{3,0,2,1:T(4,128)S(1)} %get-tuple-element.45) | copy-start | bytes 24580
  61.0 13.0 %copy-start.4 = (bf16[32,3,4096]{2,0,1:T(8,128)(2,1)S(1)}, bf16[32,3,4096]{2,0,1:T(8,128)(2,1)}, u32[]{:S(2)}) copy-start(bf16[32,3,4096]{2,0,1:T(8,128)(2,1)} %param.25) | copy-start | bytes 2359300
  74.1 2.2 %slice-start = ((s8[4456448]{0:T(1024)(128)(4,1)}), s8[4194304]{0:T(1024)(128)(4,1)S(1)}, s32[]{:S(2)}) async-start(s8[4456448]{0:T(1024)(128)(4,1)} %bitcast.153), calls=%async_computation.5 | async-start | bytes 8388608
  78.2 1.7 %collective-permute-start = (f32[4,32,544]{2,1,0:T(8,128)S(1)}, f32[4,32,544]{2,1,0:T(8,128)S(1)}, u32[]{:S(2)}, u32[]{:S(2)}) collective-permute-start(f32[4,32,544]{2,1,0:T(8,128)S(1)} %fusion), channel_id=1, source_target_pairs={{0,1},{1,0},{2,3},{3,2},{4,5},{5,4},{6,7},{7,6},{8,9},{9,8},{10,11... | collective-permute-start | bytes 835592 | tf_op jit(solution)/shard_map/ppermute | solution.py:54
  78.4 3.1 %copy-start = (bf16[32,128,2,128]{3,2,1,0:T(2,128)(2,1)S(1)}, bf16[32,128,2,128]{3,2,1,0:T(2,128)(2,1)}, u32[]{:S(2)}) copy-start(bf16[32,128,2,128]{3,2,1,0:T(2,128)(2,1)} %reshape_squeeze.6) | copy-start | bytes 6291460
  78.4 3.1 %copy-start.6 = (f32[4,32,2,8]{3,0,2,1:T(4,128)S(1)}, f32[4,32,2,8]{3,0,2,1:T(4,128)}, u32[]{:S(2)}) copy-start(f32[4,32,2,8]{3,0,2,1:T(4,128)} %copy-done.5) | copy-start | bytes 24580
  80.0 10.1 %collective-permute-start.1 = (f32[4,32,544]{2,1,0:T(8,128)S(1)}, f32[4,32,544]{2,1,0:T(8,128)}, u32[]{:S(2)}, u32[]{:S(2)}) collective-permute-start(f32[4,32,544]{2,1,0:T(8,128)S(1)} %add.111), channel_id=1, source_target_pairs={{0,2},{1,3},{2,0},{3,1},{4,6},{5,7},{6,4},{7,5},{8,10},{9,11},{10,... | collective-permute-start | bytes 835592 | tf_op jit(solution)/shard_map/ppermute | solution.py:54
  84.4 6.8 %copy-start.23 = (f32[4096]{0:T(1024)S(1)}, f32[4096]{0:T(1024)}, u32[]{:S(2)}) copy-start(f32[4096]{0:T(1024)} %param.33) | copy-start | bytes 49156
  84.4 6.8 %copy-start.24 = (f32[512]{0:T(512)S(1)}, f32[512]{0:T(512)}, u32[]{:S(2)}) copy-start(f32[512]{0:T(512)} %param.31) | copy-start | bytes 6148
  85.9 28.2 %all-to-all-start.2 = ((bf16[4,32,2048]{2,0,1:T(4,128)(2,1)}), bf16[4,32,2048]{2,0,1:T(4,128)(2,1)S(1)}, u32[]{:S(2)}, u32[]{:S(2)}) async-start(bf16[4,32,2048]{2,0,1:T(4,128)(2,1)} %copy.79), calls=%async_computation.2 | async-start | bytes 1048576 | tf_op jit(solution)/shard_map/all_to_all | solution.py:60
  91.3 4.6 %slice-start.2 = ((s8[8388608]{0:T(1024)(128)(4,1)}), s8[4194304]{0:T(1024)(128)(4,1)S(1)}, s32[]{:S(2)}) async-start(s8[8388608]{0:T(1024)(128)(4,1)} %bitcast.172), calls=%async_computation.7 | async-start | bytes 8388608
  97.6 14.0 %copy-start.18 = (f32[4096]{0:T(1024)S(1)}, f32[4096]{0:T(1024)}, u32[]{:S(2)}) copy-start(f32[4096]{0:T(1024)} %param.35) | copy-start | bytes 49156
  114.2 31.2 %copy-start.3 = (bf16[4,32,4096]{2,1,0:T(8,128)(2,1)S(1)}, bf16[4,32,4096]{2,1,0:T(8,128)(2,1)}, u32[]{:S(2)}) copy-start(bf16[4,32,4096]{2,1,0:T(8,128)(2,1)} %param.27) | copy-start | bytes 3145732
  114.2 31.2 %all-to-all-start.4 = ((bf16[4,32,4096]{2,0,1:T(4,128)(2,1)}), bf16[4,32,4096]{2,0,1:T(4,128)(2,1)S(1)}, u32[]{:S(2)}, u32[]{:S(2)}) async-start(bf16[4,32,4096]{2,0,1:T(4,128)(2,1)} %copy.83), calls=%async_computation.4 | async-start | bytes 2097152 | tf_op jit(solution)/shard_map/all_to_all | solution.py:60
  (13 other events, 17.1 us)

commit v2 on v1

v2 whole, which is shorter than its diff:
```python
import functools
import math

import jax
import jax.numpy as jnp
from jax import lax
from jax.experimental import pallas as pl
from jax.experimental.pallas import tpu as pltpu
from jax.sharding import PartitionSpec as P

HEAD_SIZE = 128
BLOCK_ROWS = 16
EPSILON = 1e-06
LOG2E = 1.4426950408889634
VMEM_LIMIT = 48 * 1024 * 1024
MESH = pl.DeviceIdType.MESH
ANY = pl.BlockSpec(memory_space=pl.ANY)
VMEM = pl.BlockSpec(memory_space=pltpu.VMEM)


def greet(axes):
    barrier = pltpu.get_barrier_semaphore()
    total = 0
    for name in axes:
        size = lax.axis_size(name)
        me = lax.axis_index(name)
        for step in range(1, size):
            pl.semaphore_signal(
                barrier, inc=1, device_id={name: lax.rem(me + step, size)}, device_id_type=MESH
            )
        total += size - 1
    pl.semaphore_wait(barrier, total)


def remote(src, dst, send_sem, recv_sem, axis, peer):
    return pltpu.make_async_remote_copy(
        src_ref=src,
        dst_ref=dst,
        send_sem=send_sem,
        recv_sem=recv_sem,
        device_id={axis: peer},
        device_id_type=MESH,
    )


def front_kernel(
    xb,
    qb,
    conv_rows,
    place,
    conv_weight,
    conv_bias,
    x_proj,
    dt_gain,
    conv_out,
    normed,
    coefs,
    q_out,
    x_in,
    proj_w,
    part,
    gathered,
    x_send,
    x_recv,
    q_send,
    q_recv,
    local_sem,
    rs_send,
    rs_recv,
    ag_send,
    ag_recv,
):
    n = lax.axis_size("req")
    width = lax.axis_size("tp")
    me = lax.axis_index("req")
    lane = lax.axis_index("tp")
    splits, rows, _ = place.shape
    block_width = xb.shape[2]
    local_reqs = conv_rows.shape[1]
    steps = rows // local_reqs
    taps = conv_weight.shape[0]
    rank_width = dt_gain.shape[1]
    proj_width = x_proj.shape[1]
    piece = rows // width
    weights_copy = pltpu.make_async_copy(x_proj, proj_w, local_sem.at[0])
    weights_copy.start()
    own_x = pltpu.make_async_copy(xb.at[me], x_in.at[me], local_sem.at[1])
    own_x.start()
    own_q = pltpu.make_async_copy(qb.at[me], q_out.at[me], local_sem.at[2])
    own_q.start()
    greet(("req", "tp"))
    x_copies, q_copies = [], []
    for step in range(1, n):
        peer = lax.rem(me + step, n)
        x_copies.append(
            remote(xb.at[peer], x_in.at[me], x_send.at[step], x_recv.at[step], "req", peer)
        )
        x_copies[-1].start()
    for step in range(1, n):
        peer = lax.rem(me + step, n)
        q_copies.append(
            remote(qb.at[peer], q_out.at[me], q_send.at[step], q_recv.at[step], "req", peer)
        )
        q_copies[-1].start()
    part[...] = jnp.zeros_like(part)
    own_x.wait()
    weights_copy.wait()
    for copy in x_copies:
        copy.wait()
    chunk = min(512, block_width)
    for split in range(splits):

        def one_chunk(at, carry):
            inner = pl.ds(pl.multiple_of(at * chunk, chunk), chunk)
            outer = pl.ds(pl.multiple_of(split * block_width + at * chunk, chunk), chunk)
            block = x_in[:, :, inner].reshape(n * BLOCK_ROWS, chunk)
            fresh = jnp.dot(place[split], block, preferred_element_type=jnp.float32)
            window = [conv_rows[row, :, outer].astype(jnp.float32) for row in range(taps - 1)]
            window += [fresh[t * local_reqs : (t + 1) * local_reqs] for t in range(steps)]
            for t in range(steps):
                total = conv_bias[:, outer] + sum(
                    conv_weight[tap : tap + 1, outer] * window[t + tap] for tap in range(taps)
                )
                active = total / (1.0 + jnp.exp(-total))
                conv_out[t * local_reqs : (t + 1) * local_reqs, outer] = active.astype(jnp.bfloat16)
            part[:, :proj_width] += jnp.dot(
                conv_out[:, outer], proj_w[outer, :], preferred_element_type=jnp.float32
            )
            return carry

        lax.fori_loop(0, block_width // chunk, one_chunk, 0)
    copies = []
    for step in range(1, width):
        peer = lax.rem(lane + step, width)
        copies.append(
            remote(
                part.at[pl.ds(pl.multiple_of(peer * piece, piece), piece)],
                gathered.at[step],
                rs_send.at[step],
                rs_recv.at[step],
                "tp",
                peer,
            )
        )
        copies[-1].start()
    mine = pl.ds(pl.multiple_of(lane * piece, piece), piece)
    gathered[0] = part[mine, :]
    for copy in copies:
        copy.wait()
    summed = gathered[0]
    for step in range(1, width):
        summed = summed + gathered[step]
    dt_low = summed[:, :rank_width]
    scale = lax.rsqrt(jnp.mean(dt_low * dt_low, axis=-1, keepdims=True) + EPSILON)
    normed[mine, :] = (dt_low * scale * dt_gain[...]).astype(jnp.bfloat16)
    coefs[mine, :] = summed[:, rank_width:]
    copies = []
    for step in range(1, width):
        peer = lax.rem(lane + step, width)
        for at, ref in enumerate((normed, coefs)):
            copies.append(
                remote(
                    ref.at[mine], ref.at[mine], ag_send.at[at, step], ag_recv.at[at, step], "tp", peer
                )
            )
            copies[-1].start()
    for copy in copies:
        copy.wait()
    own_q.wait()
    for copy in q_copies:
        copy.wait()


def front(xb, qb, conv_rows, place, conv_weight, conv_bias, x_proj, dt_gain):
    n = xb.shape[0]
    width = lax.axis_size("tp")
    rows = place.shape[1]
    channels = conv_weight.shape[1]
    rank_width = dt_gain.shape[1]
    wide = rank_width + 128
    dma = pltpu.SemaphoreType.DMA
    return pl.pallas_call(
        front_kernel,
        out_shape=(
            jax.ShapeDtypeStruct((rows, channels), jnp.bfloat16),
            jax.ShapeDtypeStruct((rows, rank_width), jnp.bfloat16),
            jax.ShapeDtypeStruct((rows, 128), jnp.float32),
            jax.ShapeDtypeStruct(qb.shape, qb.dtype),
        ),
        in_specs=[ANY, ANY, VMEM, VMEM, VMEM, VMEM, ANY, VMEM],
        out_specs=(VMEM, VMEM, VMEM, ANY),
        scratch_shapes=[
            pltpu.VMEM(xb.shape, xb.dtype),
            pltpu.VMEM(x_proj.shape, x_proj.dtype),
            pltpu.VMEM((rows, wide), jnp.float32),
            pltpu.VMEM((width, rows // width, wide), jnp.float32),
            dma((n,)),
            dma((n,)),
            dma((n,)),
            dma((n,)),
            dma((3,)),
            dma((width,)),
            dma((width,)),
            dma((2, width)),
            dma((2, width)),
        ],
        compiler_params=pltpu.CompilerParams(
            collective_id=0, has_side_effects=True, vmem_limit_bytes=VMEM_LIMIT
        ),
    )(xb, qb, conv_rows, place, conv_weight, conv_bias, x_proj, dt_gain)


def attention_kernel(
    kv_heads, q_rows, steps, table, lengths, slots, slabs, pool, out, pages, page_sem
):
    local_reqs, list_len = table.shape
    page_tokens = pool.shape[2]
    cache_len = list_len * page_tokens
    scale = 1.0 / math.sqrt(HEAD_SIZE)
    recent = kv_heads * steps
    group_width = q_rows // steps

    def fetch(req, carry):
        for at in range(list_len):
            pltpu.make_async_copy(
                pool.at[table[req, at]], pages.at[req, at], page_sem.at[req]
            ).start()
        return carry

    lax.fori_loop(0, local_reqs, fetch, 0)
    token = lax.broadcasted_iota(jnp.int32, (q_rows, cache_len), 1)
    column = lax.broadcasted_iota(jnp.int32, (q_rows, recent), 1)
    moment = lax.broadcasted_iota(jnp.int32, (q_rows, recent), 0) // group_width

    def one_request(req):
        pltpu.make_async_copy(
            pool.at[pl.ds(0, list_len)], pages.at[req], page_sem.at[req]
        ).wait()
        slot = slots[req]
        valid = token < lengths[req]
        base = kv_heads * q_rows
        new_keys = slabs[slot, base : base + recent, :]
        new_values = slabs[slot, base + recent : base + 2 * recent, :]
        for head in range(kv_heads):
            cols = slice(head * HEAD_SIZE, (head + 1) * HEAD_SIZE)
            query = slabs[slot, head * q_rows : (head + 1) * q_rows, :]
            keys = pages[req, :, 0, :, cols].reshape(cache_len, HEAD_SIZE)
            values = pages[req, :, 1, :, cols].reshape(cache_len, HEAD_SIZE)
            contract = (((1,), (1,)), ((), ()))
            old = lax.dot_general(query, keys, contract, preferred_element_type=jnp.float32)
            new = lax.dot_general(query, new_keys, contract, preferred_element_type=jnp.float32)
            seen = (column >= head * steps) & (column <= head * steps + moment)
            old = jnp.where(valid, old * scale, -jnp.inf)
            new = jnp.where(seen, new * scale, -jnp.inf)
            top = jnp.maximum(
                jnp.max(old, axis=1, keepdims=True), jnp.max(new, axis=1, keepdims=True)
            )
            old = jnp.exp(old - top)
            new = jnp.exp(new - top)
            total = jnp.sum(old, axis=1, keepdims=True) + jnp.sum(new, axis=1, keepdims=True)
            mixed = jnp.dot(
                old.astype(jnp.bfloat16), values, preferred_element_type=jnp.float32
            ) + jnp.dot(new.astype(jnp.bfloat16), new_values, preferred_element_type=jnp.float32)
            out[slot, head * q_rows : (head + 1) * q_rows, :] = (mixed / total).astype(jnp.bfloat16)

    unroll = 4

    def some_requests(at, carry):
        for offset in range(unroll):
            one_request(at * unroll + offset)
        return carry

    lax.fori_loop(0, local_reqs // unroll, some_requests, 0)


def attention(slabs, pool, table, lengths, slots, kv_heads, q_rows, steps):
    local_reqs, list_len = table.shape
    smem = pl.BlockSpec(memory_space=pltpu.SMEM)
    return pl.pallas_call(
        functools.partial(attention_kernel, kv_heads, q_rows, steps),
        out_shape=jax.ShapeDtypeStruct((local_reqs, kv_heads * q_rows, HEAD_SIZE), jnp.bfloat16),
        in_specs=[smem, smem, smem, VMEM, ANY],
        out_specs=VMEM,
        scratch_shapes=[
            pltpu.VMEM((local_reqs, list_len) + pool.shape[1:], pool.dtype),
            pltpu.SemaphoreType.DMA((local_reqs,)),
        ],
        compiler_params=pltpu.CompilerParams(vmem_limit_bytes=VMEM_LIMIT),
    )(table, lengths, slots, slabs, pool)


def scan_chunk_of(block_width):
    return min(512, block_width)


def back_kernel(
    ob,
    conv_out,
    normed,
    coefs,
    place_back,
    dt_proj,
    dt_bias,
    a_log,
    skip_d,
    state,
    o_out,
    y_out,
    held,
    rate_w,
    rates,
    drives,
    readings,
    ready,
    o_send,
    o_recv,
    y_send,
    y_recv,
    local_sem,
    chunk_sem,
):
    n = lax.axis_size("req")
    me = lax.axis_index("req")
    splits, _, rows = place_back.shape
    local_reqs, state_size, channels = state.shape
    steps = rows // local_reqs
    block_width = channels // splits
    chunk = scan_chunk_of(block_width)
    chunks = block_width // chunk
    for w_at in range(chunks):
        for split in range(splits):
            at = split * chunks + w_at
            cols = pl.ds(at * chunk, chunk)
            pltpu.make_async_copy(dt_proj.at[:, cols], rate_w.at[:, cols], chunk_sem.at[0, at]).start()
            pltpu.make_async_copy(
                state.at[:, :, cols], held.at[:, :, cols], chunk_sem.at[1, at]
            ).start()
    own_o = pltpu.make_async_copy(ob.at[me], o_out.at[me], local_sem.at[0])
    own_o.start()
    greet(("req",))
    o_copies = []
    for step in range(1, n):
        peer = lax.rem(me + step, n)
        o_copies.append(
            remote(ob.at[peer], o_out.at[me], o_send.at[step], o_recv.at[step], "req", peer)
        )
        o_copies[-1].start()

    def one_chunk(w_at, carry):
        inner = pl.ds(pl.multiple_of(w_at * chunk, chunk), chunk)
        blocks = jnp.zeros((n * BLOCK_ROWS, chunk), jnp.float32)
        for split in range(splits):
            at = split * chunks + w_at
            outer = pl.ds(pl.multiple_of(at * chunk, chunk), chunk)
            pltpu.make_async_copy(
                dt_proj.at[:, outer], rate_w.at[:, outer], chunk_sem.at[0, at]
            ).wait()
            raw = (
                jnp.dot(normed[...], rate_w[:, outer], preferred_element_type=jnp.float32)
                + dt_bias[:, outer]
            )
            rate = jnp.maximum(raw, 0.0) + jnp.log1p(jnp.exp(-jnp.abs(raw)))
            inputs = conv_out[:, outer].astype(jnp.float32)
            rates[...] = rate
            drives[...] = rate * inputs
            decay = jnp.exp(a_log[:, outer]) * (-LOG2E)
            pltpu.make_async_copy(
                state.at[:, :, outer], held.at[:, :, outer], chunk_sem.at[1, at]
            ).wait()

            def one_request(req, inner_carry):
                hidden = held[req, :, outer]
                pair = coefs[req]
                for t in range(steps):
                    row = pl.ds(t * local_reqs + req, 1)
                    hidden = jnp.exp2(rates[row, :] * decay) * hidden + drives[row, :] * pair[:, t : t + 1]
                    readings[row, :] = jnp.sum(
                        hidden * pair[:, steps + t : steps + t + 1], axis=0, keepdims=True
                    )
                return inner_carry

            lax.fori_loop(0, local_reqs, one_request, 0)
            reading = (readings[...] + skip_d[:, outer] * inputs).astype(jnp.bfloat16)
            blocks = blocks + jnp.dot(
                place_back[split], reading, preferred_element_type=jnp.float32
            )
        ready[:, :, inner] = blocks.astype(jnp.bfloat16).reshape(n, BLOCK_ROWS, chunk)
        for step in range(1, n):
            peer = lax.rem(me + step, n)
            remote(
                ready.at[peer, :, inner],
                y_out.at[me, :, inner],
                y_send.at[step],
                y_recv.at[step],
                "req",
                peer,
            ).start()
        return carry

    lax.fori_loop(0, chunks, one_chunk, 0)
    own_y = pltpu.make_async_copy(ready.at[me], y_out.at[me], local_sem.at[1])
    own_y.start()
    own_o.wait()
    for copy in o_copies:
        copy.wait()
    for step in range(1, n):
        peer = lax.rem(me + step, n)
        remote(
            ready.at[peer], y_out.at[me], y_send.at[step], y_recv.at[step], "req", peer
        ).wait()
    own_y.wait()


def back(ob, conv_out, normed, coefs, place_back, dt_proj, dt_bias, a_log, skip_d, state):
    n = ob.shape[0]
    splits, block_total, rows = place_back.shape
    channels = state.shape[2]
    block_width = channels // splits
    chunk = scan_chunk_of(block_width)
    dma = pltpu.SemaphoreType.DMA
    blocks = (n, BLOCK_ROWS, block_width)
    return pl.pallas_call(
        back_kernel,
        out_shape=(
            jax.ShapeDtypeStruct(ob.shape, ob.dtype),
            jax.ShapeDtypeStruct(blocks, jnp.bfloat16),
        ),
        in_specs=[ANY, VMEM, VMEM, VMEM, VMEM, ANY, VMEM, VMEM, VMEM, ANY],
        out_specs=(ANY, ANY),
        scratch_shapes=[
            pltpu.VMEM(state.shape, state.dtype),
            pltpu.VMEM(dt_proj.shape, dt_proj.dtype),
            pltpu.VMEM((rows, chunk), jnp.float32),
            pltpu.VMEM((rows, chunk), jnp.float32),
            pltpu.VMEM((rows, chunk), jnp.float32),
            pltpu.VMEM(blocks, jnp.bfloat16),
            dma((n,)),
            dma((n,)),
            dma((n,)),
            dma((n,)),
            dma((2,)),
            dma((2, channels // chunk)),
        ],
        compiler_params=pltpu.CompilerParams(
            collective_id=1, has_side_effects=True, vmem_limit_bytes=VMEM_LIMIT
        ),
    )(ob, conv_out, normed, coefs, place_back, dt_proj, dt_bias, a_log, skip_d, state)


def per_device(
    queries,
    new_kv,
    prefill_page_pool,
    page_table,
    prompt_len,
    dest_device,
    ssm_state,
    conv_state,
    mamba_x,
    mamba_z,
    conv_weight,
    conv_bias,
    x_proj,
    dt_gain,
    dt_proj,
    dt_bias,
    a_log,
    skip_d,
):
    n = lax.axis_size("req")
    local_reqs = dest_device.shape[0]
    steps = queries.shape[0]
    channels = mamba_x.shape[2]
    kv_heads = prefill_page_pool.shape[3] // HEAD_SIZE
    group_width = queries.shape[2] // HEAD_SIZE // kv_heads
    q_rows = steps * group_width
    state_size = a_log.shape[0]
    share = local_reqs // n
    splits = BLOCK_ROWS // (steps * share)
    block_width = channels // splits
    index = jnp.arange(local_reqs, dtype=jnp.int32)
    same = dest_device[:, None] == dest_device[None, :]
    rank = jnp.sum((same & (index[None, :] < index[:, None])).astype(jnp.int32), axis=1)
    slots = dest_device * share + rank
    times = jnp.arange(steps, dtype=jnp.int32)
    split_ids = jnp.arange(splits, dtype=jnp.int32)
    block_row = dest_device * BLOCK_ROWS + rank * splits
    block_row = (
        block_row[None, None, :]
        + times[None, :, None] * (share * splits)
        + split_ids[:, None, None]
    ).reshape(splits, steps * local_reqs)
    block_ids = jnp.arange(n * BLOCK_ROWS, dtype=jnp.int32)
    place = (block_row[:, :, None] == block_ids[None, None, :]).astype(jnp.bfloat16)
    place_back = (block_row[:, None, :] == block_ids[None, :, None]).astype(jnp.bfloat16)

    xb = jnp.transpose(
        mamba_x.reshape(steps, n, share, channels), (1, 0, 2, 3)
    ).reshape(n, BLOCK_ROWS, block_width)
    q_part = jnp.transpose(
        queries.reshape(steps, local_reqs, kv_heads, group_width, HEAD_SIZE), (1, 2, 0, 3, 4)
    ).reshape(local_reqs, kv_heads * q_rows, HEAD_SIZE)
    kv_part = jnp.transpose(
        new_kv.reshape(steps, local_reqs, 2, kv_heads, HEAD_SIZE), (1, 2, 3, 0, 4)
    ).reshape(local_reqs, 2 * kv_heads * steps, HEAD_SIZE)
    slabs = jnp.concatenate([q_part, kv_part], axis=1)
    slab_rows = slabs.shape[1]
    conv_out, normed, coefs, slabs = front(
        xb,
        slabs.reshape(n, share * slab_rows, HEAD_SIZE),
        jnp.transpose(conv_state, (1, 0, 2)),
        place,
        conv_weight,
        conv_bias[None],
        x_proj,
        dt_gain[None],
    )
    ob = attention(
        slabs.reshape(local_reqs, slab_rows, HEAD_SIZE),
        prefill_page_pool,
        page_table,
        prompt_len,
        slots,
        kv_heads,
        q_rows,
        steps,
    )
    coefs = jnp.transpose(
        coefs[:, : 2 * state_size].reshape(steps, local_reqs, 2, state_size), (1, 3, 2, 0)
    ).reshape(local_reqs, state_size, 2 * steps)
    o_back, y_back = back(
        ob.reshape(n, share * kv_heads * q_rows, HEAD_SIZE),
        conv_out,
        normed,
        coefs,
        place_back,
        dt_proj,
        dt_bias[None],
        a_log,
        skip_d[None],
        ssm_state,
    )
    attn_out = jnp.transpose(
        o_back.reshape(local_reqs, kv_heads, steps, group_width, HEAD_SIZE), (2, 0, 1, 3, 4)
    ).reshape(queries.shape)
    reading = jnp.transpose(
        y_back.reshape(n, steps, share, channels), (1, 0, 2, 3)
    ).reshape(mamba_x.shape)
    gate_values = jax.nn.silu(mamba_z.astype(jnp.float32))
    mamba_out = (reading.astype(jnp.float32) * gate_values).astype(jnp.bfloat16)
    return (attn_out, mamba_out)


def solution(mesh):
    return jax.shard_map(
        per_device,
        mesh=mesh,
        in_specs=(
            P(None, "req", "tp"),
            P(None, "req", None, "tp"),
            P("req", None, None, "tp"),
            P("req", None),
            P("req"),
            P("req"),
            P("req", None, "tp"),
            P("req", None, "tp"),
            P(None, "req", "tp"),
            P(None, "req", "tp"),
            P(None, "tp"),
            P("tp"),
            P("tp", None),
            P(),
            P(None, "tp"),
            P("tp"),
            P(None, "tp"),
            P("tp"),
        ),
        out_specs=(P(None, "req", "tp"), P(None, "req", "tp")),
        check_vma=False,
    )
```

time: 148 us -> 152 us (1.027)
  Pallas kernels: 0 us -> 119 us
  waiting for transfers between devices: 46.2 us -> 0 us
  starting transfers between devices: 27.6 us -> 0 us
  other arithmetic: 22.3 us -> 4.49 us
  matrix products: 17.5 us -> 0 us
  local copies, waits for them, and re-layouts: 32.5 us -> 27 us
    pallas_call x0 -> x3, Pallas kernels: none -> 119 us  [the longest x1 50.4 us: back(): pl.pallas_call(back_kernel, out_shape=(jax.ShapeDtypeStruct(ob.shape, ob....]
    all_to_all x5 -> x0, waiting for transfers between devices: 45.4 us -> none  [swap_rows(): return lax.all_to_all(value, 'req', split_axis=1, concat_axis=1, tiled=True)]
    all_to_all x5 -> x0, starting transfers between devices: 26 us -> none  [swap_rows(): return lax.all_to_all(value, 'req', split_axis=1, concat_axis=1, tiled=True)]
    dot_general x11 -> x0, matrix products: 17.5 us -> none  [the longest x1 4.11 us: mamba_readings(): jnp.einsum('trk,kc->trc', normed, dt_proj, preferred_element_type=jnp.flo...]
    reduce_sum x4 -> x0, other arithmetic: 16 us -> none  [the longest x1 14 us: mamba_readings(): jnp.sum(c_coef[moment][:, :, None] * hidden_state, axis=1)]
    another operation x2 -> x0, local copies, waits for them, and re-layouts: 6.01 us -> none  [the longest x1 3.96 us: per_device(): picked[:, :, 0].reshape(local_reqs, cache_len, kv_heads, HEAD_SIZE)]
    unnamed x65 -> x47, local copies, waits for them, and re-layouts: 13.6 us -> 19.3 us
    gather x1 -> x0, local copies, waits for them, and re-layouts: 4.95 us -> none  [per_device(): picked = prefill_page_pool[page_table]]
  transfers between devices with their start and end apart: 7 -> 0, of which waited for: 5 -> 0; matrix products, arithmetic and copies ran while one was open for 41% -> 0% of each run, Pallas kernels for 0% -> 0%
where the time goes in v2:
time: 152 us; the launch traced here: 151 us
  Pallas kernels  119 us (78%)
  local copies, waits for them, and re-layouts  27 us (18%)
  other arithmetic  4.49 us (3%)
    pallas_call x1, Pallas kernels, back(): pl.pallas_call(back_kernel, out_shape=(jax.ShapeDtypeStruct(ob.shape, ob....  50.4 us
    pallas_call x1, Pallas kernels, front(): pl.pallas_call(front_kernel, out_shape=(jax.ShapeDtypeStruct((rows, chann...  40.2 us
    pallas_call x1, Pallas kernels, attention(): pl.pallas_call(functools.partial(attention_kernel, kv_heads, q_rows, step...  28 us
    unnamed x47, local copies, waits for them, and re-layouts  19.3 us
    convert_element_type x3, local copies, waits for them, and re-layouts, per_device(): mamba_out = (reading.astype(jnp.float32) * gate_values).astype(jnp.bfloat16)  4.21 us

profile of v2, /device:TPU:0, one launch (start us, length us, event | category | flops | bytes accessed | tf_op | source)
XLA Modules:
  0.0 151.0 jit_solution(9641006375765782680)
XLA Ops:
  0.6 0.9 convert_reduce_fusion
  1.5 1.2 multiply_add_fusion
  3.0 0.7 fusion.6
  3.8 7.6 %copy.41.x_proj = bf16[4096,544]{1,0:T(8,128)(2,1)} copy(bf16[4096,544]{0,1:T(8,128)(2,1)} %param.30) | data formatting | bytes 8912896 | tf_op args[12]
  13.9 0.8 copy-done.8
  14.7 0.8 copy-done.9
  15.5 0.7 copy-done.15
  16.2 40.2 %shard_map.185 = (bf16[128,4096]{1,0:T(8,128)(2,1)S(1)}, bf16[128,512]{1,0:T(8,128)(2,1)S(1)}, f32[128,128]{1,0:T(8,128)S(1)}, bf16[8,320,128]{2,1,0:T(8,128)(2,1)S(1)}) custom-call(bf16[8,16,4096]{2,1,0:T(8,128)(2,1)S(1)} %reshape.167.xb, bf16[8,320,128]{2,1,0:T(8,128)(2,1)S(1)} %bitcast.33, bf16[3,32,4096]{2,1,0:T(8,128)(2,1)S(1)} %bitcast.35, ...), custom_call_target="tpu_custom_call" | custom-call | tf_op jit(solution)/shard_map/pallas_call | solution.py:182
  56.5 0.6 copy-done.5
  57.7 0.8 copy.42.table
  58.5 2.2 %copy-done = bf16[256,2,16,256]{3,2,1,0:T(8,128)(2,1)S(1)} copy-done((bf16[256,2,16,256]{3,2,1,0:T(8,128)(2,1)S(1)}, bf16[256,2,16,256]{3,2,1,0:T(8,128)(2,1)}, u32[]{:S(2)}) %copy-start) | copy-done | bytes 4194328
  60.7 0.7 copy-done.16
  61.4 0.7 copy-done.17
  62.0 28.0 %shard_map.186 = bf16[32,64,128]{2,1,0:T(8,128)(2,1)S(1)} custom-call(s32[32,8]{1,0:T(8,128)S(1)} %copy.42.table, s32[32]{0:T(128)S(1)} %copy-done.17, s32[32]{0:T(128)S(1)} %copy-done.16, bf16[32,80,128]{2,1,0:T(8,128)(2,1)S(1)} %bitcast.36, bf16[256,2,16,256]{3,2,1,0:T(8,128)(2,1)S(1)} %copy-done), custom_call_target="tpu_custom_call" | custom-call | tf_op jit(solution)/shard_map/pallas_call | solution.py:279
  90.5 0.9 copy-done.6
  91.4 0.8 copy-done.7
  92.1 0.7 copy-done.14
  92.8 50.4 %shard_map.187 = (bf16[8,256,128]{2,1,0:T(8,128)(2,1)S(1)}, bf16[8,16,4096]{2,1,0:T(8,128)(2,1)S(1)}) custom-call(bf16[8,256,128]{2,1,0:T(8,128)(2,1)S(1)} %bitcast.34, bf16[128,4096]{1,0:T(8,128)(2,1)S(1)} %get-tuple-element.9.conv_out, bf16[128,512]{1,0:T(8,128)(2,1)S(1)} %copy-done.6, f32[32,16,8]{2,1,0:T(8,128)S(1)} %copy.45.coefs, ...), custom_call_target="tpu_custom_call" | custom-call | tf_op jit(solution)/shard_map/pallas_call | solution.py:422
  143.3 0.8 copy-done.2
  144.0 0.7 reshape.180
  144.7 1.5 copy.47
  146.2 2.1 %reshape.179 = f32[4,32,4096]{2,1,0:T(8,128)S(1)} reshape(f32[4,8,4,4096]{3,2,1,0:T(4,128)} %copy.47) | data formatting | bytes 4194304 | tf_op jit(solution)/shard_map/convert_element_type | solution.py:550
  148.3 1.6 %fusion.4 = bf16[4,32,4096]{2,1,0:T(8,128)(2,1)} fusion(f32[4,32,4096]{2,1,0:T(8,128)S(1)} %reshape.179, bf16[4,32,4096]{2,1,0:T(8,128)(2,1)S(1)} %copy-done.19), kind=kLoop, calls=%fused_computation.6 | loop fusion | flops 3670016 | bytes 4194304 | tf_op jit(solution)/shard_map/convert_element_type | solution.py:550
  150.0 1.0 reshape.178
  (52 shorter events, 3.8 us)
Async XLA Ops:
  3.8 7.6 %copy-start.18 = (bf16[4,32,4096]{2,1,0:T(8,128)(2,1)S(1)}, bf16[4,32,4096]{2,1,0:T(8,128)(2,1)}, u32[]{:S(2)}) copy-start(bf16[4,32,4096]{2,1,0:T(8,128)(2,1)} %param.26) | copy-start | bytes 3145732
  11.8 1.0 copy-start.20
  12.4 0.9 copy-start.21
  12.7 1.2 copy-start.1
  12.8 1.2 copy-start.12
  13.9 0.8 copy-start.8
  14.7 0.8 copy-start.9
  15.5 0.7 copy-start.15
  56.5 0.7 copy-start.5
  57.1 0.6 copy-start.10
  58.5 2.2 %copy-start = (bf16[256,2,16,256]{3,2,1,0:T(8,128)(2,1)S(1)}, bf16[256,2,16,256]{3,2,1,0:T(8,128)(2,1)}, u32[]{:S(2)}) copy-start(bf16[256,2,16,256]{3,2,1,0:T(8,128)(2,1)} %pool.1) | copy-start | bytes 12582916
  60.7 0.7 copy-start.16
  61.4 0.7 copy-start.17
  62.0 28.0 %copy-start.11 = (f32[128,128]{1,0:T(8,128)S(1)}, f32[128,128]{1,0:T(8,128)}, u32[]{:S(2)}) copy-start(f32[128,128]{1,0:T(8,128)} %copy-done.10) | copy-start | bytes 196612
  62.0 28.4 %copy-start.4 = (f32[16,4096]{1,0:T(8,128)S(1)}, f32[16,4096]{1,0:T(8,128)}, u32[]{:S(2)}) copy-start(f32[16,4096]{1,0:T(8,128)} %a_log.1) | copy-start | bytes 786436
  62.0 28.4 %copy-start.13 = (f32[4096]{0:T(1024)S(1)}, f32[4096]{0:T(1024)}, u32[]{:S(2)}) copy-start(f32[4096]{0:T(1024)} %param.33) | copy-start | bytes 49156
  90.5 0.9 copy-start.6
  91.4 0.8 copy-start.7
  92.1 0.7 copy-start.14
  143.3 0.8 copy-start.2
  146.2 2.1 %copy-start.19 = (bf16[4,32,4096]{2,1,0:T(8,128)(2,1)S(1)}, bf16[4,32,4096]{2,1,0:T(8,128)(2,1)}, u32[]{:S(2)}) copy-start(bf16[4,32,4096]{2,1,0:T(8,128)(2,1)} %param.27) | copy-start | bytes 3145732
  148.3 1.6 %copy-start.3 = (bf16[8,256,128]{2,1,0:T(8,128)(2,1)S(1)}, bf16[8,256,128]{2,1,0:T(8,128)(2,1)}, u32[]{:S(2)}) copy-start(bf16[8,256,128]{2,1,0:T(8,128)(2,1)} %copy-done.2) | copy-start | bytes 1572868

commit v3 on v2

--- a/solution.py
+++ b/solution.py
@@ -12,7 +12,7 @@
 BLOCK_ROWS = 16
 EPSILON = 1e-06
 LOG2E = 1.4426950408889634
-VMEM_LIMIT = 48 * 1024 * 1024
+VMEM_LIMIT = 56 * 1024 * 1024
 MESH = pl.DeviceIdType.MESH
 ANY = pl.BlockSpec(memory_space=pl.ANY)
 VMEM = pl.BlockSpec(memory_space=pltpu.VMEM)
@@ -43,19 +43,38 @@
     )
 
 
+def bring(sems, *pairs):
+    copies = [
+        pltpu.make_async_copy(src, dst, sems.at[at]) for at, (src, dst) in enumerate(pairs)
+    ]
+    for copy in copies:
+        copy.start()
+    return copies
+
+
+def like(value):
+    return pltpu.VMEM(value.shape, value.dtype)
+
+
 def front_kernel(
     xb,
     qb,
+    conv_rows_far,
+    place_far,
+    conv_weight_far,
+    conv_bias_far,
+    x_proj,
+    dt_gain_far,
+    conv_out,
+    normed,
+    coefs,
+    q_out,
     conv_rows,
     place,
     conv_weight,
     conv_bias,
-    x_proj,
     dt_gain,
-    conv_out,
-    normed,
-    coefs,
-    q_out,
+    load_sem,
     x_in,
     proj_w,
     part,
@@ -80,8 +99,16 @@
     steps = rows // local_reqs
     taps = conv_weight.shape[0]
     rank_width = dt_gain.shape[1]
-    proj_width = x_proj.shape[1]
+    proj_width = x_proj.shape[0]
     piece = rows // width
+    loads = bring(
+        load_sem,
+        (conv_rows_far, conv_rows),
+        (place_far, place),
+        (conv_weight_far, conv_weight),
+        (conv_bias_far, conv_bias),
+        (dt_gain_far, dt_gain),
+    )
     weights_copy = pltpu.make_async_copy(x_proj, proj_w, local_sem.at[0])
     weights_copy.start()
     own_x = pltpu.make_async_copy(xb.at[me], x_in.at[me], local_sem.at[1])
@@ -96,17 +123,19 @@
             remote(xb.at[peer], x_in.at[me], x_send.at[step], x_recv.at[step], "req", peer)
         )
         x_copies[-1].start()
+    part[...] = jnp.zeros_like(part)
+    for copy in loads:
+        copy.wait()
+    own_x.wait()
+    weights_copy.wait()
+    for copy in x_copies:
+        copy.wait()
     for step in range(1, n):
         peer = lax.rem(me + step, n)
         q_copies.append(
             remote(qb.at[peer], q_out.at[me], q_send.at[step], q_recv.at[step], "req", peer)
         )
         q_copies[-1].start()
-    part[...] = jnp.zeros_like(part)
-    own_x.wait()
-    weights_copy.wait()
-    for copy in x_copies:
-        copy.wait()
     chunk = min(512, block_width)
     for split in range(splits):
 
@@ -123,8 +152,11 @@
                 )
                 active = total / (1.0 + jnp.exp(-total))
                 conv_out[t * local_reqs : (t + 1) * local_reqs, outer] = active.astype(jnp.bfloat16)
-            part[:, :proj_width] += jnp.dot(
-                conv_out[:, outer], proj_w[outer, :], preferred_element_type=jnp.float32
+            part[:, :proj_width] += lax.dot_general(
+                conv_out[:, outer],
+                proj_w[:, outer],
+                (((1,), (1,)), ((), ())),
+                preferred_element_type=jnp.float32,
             )
             return carry
 
@@ -187,9 +219,15 @@
             jax.ShapeDtypeStruct((rows, 128), jnp.float32),
             jax.ShapeDtypeStruct(qb.shape, qb.dtype),
         ),
-        in_specs=[ANY, ANY, VMEM, VMEM, VMEM, VMEM, ANY, VMEM],
+        in_specs=[ANY] * 8,
         out_specs=(VMEM, VMEM, VMEM, ANY),
         scratch_shapes=[
+            like(conv_rows),
+            like(place),
+            like(conv_weight),
+            like(conv_bias),
+            like(dt_gain),
+            dma((5,)),
             pltpu.VMEM(xb.shape, xb.dtype),
             pltpu.VMEM(x_proj.shape, x_proj.dtype),
             pltpu.VMEM((rows, wide), jnp.float32),
@@ -210,47 +248,49 @@
     )(xb, qb, conv_rows, place, conv_weight, conv_bias, x_proj, dt_gain)
 
 
-def attention_kernel(
-    kv_heads, q_rows, steps, table, lengths, slots, slabs, pool, out, pages, page_sem
-):
+def attention_kernel(kv_heads, q_rows, steps, table, lengths, slots, slabs, pool, out):
     local_reqs, list_len = table.shape
-    page_tokens = pool.shape[2]
-    cache_len = list_len * page_tokens
+    cache_len = list_len * pool.shape[2]
     scale = 1.0 / math.sqrt(HEAD_SIZE)
     recent = kv_heads * steps
+    all_rows = kv_heads * q_rows
     group_width = q_rows // steps
-
-    def fetch(req, carry):
-        for at in range(list_len):
-            pltpu.make_async_copy(
-                pool.at[table[req, at]], pages.at[req, at], page_sem.at[req]
-            ).start()
-        return carry
-
-    lax.fori_loop(0, local_reqs, fetch, 0)
-    token = lax.broadcasted_iota(jnp.int32, (q_rows, cache_len), 1)
-    column = lax.broadcasted_iota(jnp.int32, (q_rows, recent), 1)
-    moment = lax.broadcasted_iota(jnp.int32, (q_rows, recent), 0) // group_width
-
-    def one_request(req):
-        pltpu.make_async_copy(
-            pool.at[pl.ds(0, list_len)], pages.at[req], page_sem.at[req]
-        ).wait()
-        slot = slots[req]
-        valid = token < lengths[req]
-        base = kv_heads * q_rows
-        new_keys = slabs[slot, base : base + recent, :]
-        new_values = slabs[slot, base + recent : base + 2 * recent, :]
-        for head in range(kv_heads):
-            cols = slice(head * HEAD_SIZE, (head + 1) * HEAD_SIZE)
-            query = slabs[slot, head * q_rows : (head + 1) * q_rows, :]
-            keys = pages[req, :, 0, :, cols].reshape(cache_len, HEAD_SIZE)
-            values = pages[req, :, 1, :, cols].reshape(cache_len, HEAD_SIZE)
-            contract = (((1,), (1,)), ((), ()))
-            old = lax.dot_general(query, keys, contract, preferred_element_type=jnp.float32)
-            new = lax.dot_general(query, new_keys, contract, preferred_element_type=jnp.float32)
-            seen = (column >= head * steps) & (column <= head * steps + moment)
-            old = jnp.where(valid, old * scale, -jnp.inf)
+    token = lax.broadcasted_iota(jnp.int32, (all_rows, cache_len), 1)
+    column = lax.broadcasted_iota(jnp.int32, (all_rows, recent), 1)
+    row = lax.broadcasted_iota(jnp.int32, (all_rows, recent), 0)
+    row_head = row // q_rows
+    row_moment = (row - row_head * q_rows) // group_width
+    seen = (column >= row_head * steps) & (column <= row_head * steps + row_moment)
+    contract = (((1,), (1,)), ((), ()))
+    together = 4
+
+    def some_requests(at, carry):
+        reqs = [at * together + offset for offset in range(together)]
+        rows = [slots[req] for req in reqs]
+        scores, fresh = [], []
+        for req, slot in zip(reqs, rows):
+            keys = jnp.concatenate([pool[table[req, i], 0] for i in range(list_len)], axis=0)
+            parts = [
+                lax.dot_general(
+                    slabs[slot, head * q_rows : (head + 1) * q_rows, :],
+                    keys[:, head * HEAD_SIZE : (head + 1) * HEAD_SIZE],
+                    contract,
+                    preferred_element_type=jnp.float32,
+                )
+                for head in range(kv_heads)
+            ]
+            scores.append(jnp.concatenate(parts, axis=0))
+            fresh.append(
+                lax.dot_general(
+                    slabs[slot, :all_rows, :],
+                    slabs[slot, all_rows : all_rows + recent, :],
+                    contract,
+                    preferred_element_type=jnp.float32,
+                )
+            )
+        weights = []
+        for req, old, new in zip(reqs, scores, fresh):
+            old = jnp.where(token < lengths[req], old * scale, -jnp.inf)
             new = jnp.where(seen, new * scale, -jnp.inf)
             top = jnp.maximum(
                 jnp.max(old, axis=1, keepdims=True), jnp.max(new, axis=1, keepdims=True)
@@ -258,33 +298,36 @@
             old = jnp.exp(old - top)
             new = jnp.exp(new - top)
             total = jnp.sum(old, axis=1, keepdims=True) + jnp.sum(new, axis=1, keepdims=True)
-            mixed = jnp.dot(
-                old.astype(jnp.bfloat16), values, preferred_element_type=jnp.float32
-            ) + jnp.dot(new.astype(jnp.bfloat16), new_values, preferred_element_type=jnp.float32)
-            out[slot, head * q_rows : (head + 1) * q_rows, :] = (mixed / total).astype(jnp.bfloat16)
-
-    unroll = 4
-
-    def some_requests(at, carry):
-        for offset in range(unroll):
-            one_request(at * unroll + offset)
+            weights.append((old.astype(jnp.bfloat16), new.astype(jnp.bfloat16), 1.0 / total))
+        for req, slot, (old, new, inverse) in zip(reqs, rows, weights):
+            values = jnp.concatenate([pool[table[req, i], 1] for i in range(list_len)], axis=0)
+            parts = [
+                jnp.dot(
+                    old[head * q_rows : (head + 1) * q_rows, :],
+                    values[:, head * HEAD_SIZE : (head + 1) * HEAD_SIZE],
+                    preferred_element_type=jnp.float32,
+                )
+                for head in range(kv_heads)
+            ]
+            mixed = jnp.concatenate(parts, axis=0) + jnp.dot(
+                new,
+                slabs[slot, all_rows + recent : all_rows + 2 * recent, :],
+                preferred_element_type=jnp.float32,
+            )
+            out[slot] = (mixed * inverse).astype(jnp.bfloat16)
         return carry
 
-    lax.fori_loop(0, local_reqs // unroll, some_requests, 0)
+    lax.fori_loop(0, local_reqs // together, some_requests, 0)
 
 
 def attention(slabs, pool, table, lengths, slots, kv_heads, q_rows, steps):
-    local_reqs, list_len = table.shape
+    local_reqs = table.shape[0]
     smem = pl.BlockSpec(memory_space=pltpu.SMEM)
     return pl.pallas_call(
         functools.partial(attention_kernel, kv_heads, q_rows, steps),
         out_shape=jax.ShapeDtypeStruct((local_reqs, kv_heads * q_rows, HEAD_SIZE), jnp.bfloat16),
-        in_specs=[smem, smem, smem, VMEM, ANY],
+        in_specs=[smem, smem, smem, VMEM, VMEM],
         out_specs=VMEM,
-        scratch_shapes=[
-            pltpu.VMEM((local_reqs, list_len) + pool.shape[1:], pool.dtype),
-            pltpu.SemaphoreType.DMA((local_reqs,)),
-        ],
         compiler_params=pltpu.CompilerParams(vmem_limit_bytes=VMEM_LIMIT),
     )(table, lengths, slots, slabs, pool)
 
@@ -295,17 +338,28 @@
 
 def back_kernel(
     ob,
+    conv_out_far,
+    normed_far,
+    coefs_far,
+    place_back_far,
+    dt_proj,
+    dt_bias_far,
+    a_log_far,
+    skip_d_far,
+    state,
+    o_out,
+    y_out,
     conv_out,
     normed,
     coefs,
     place_back,
-    dt_proj,
     dt_bias,
     a_log,
     skip_d,
-    state,
-    o_out,
-    y_out,
+    load_sem,
+    b_wide,
+    c_wide,
+    decay,
     held,
     rate_w,
     rates,
@@ -318,23 +372,40 @@
     y_recv,
     local_sem,
     chunk_sem,
+    state_sem,
 ):
     n = lax.axis_size("req")
     me = lax.axis_index("req")
     splits, _, rows = place_back.shape
-    local_reqs, state_size, channels = state.shape
+    state_size, channels = a_log.shape
+    local_reqs = state.shape[0] // state_size
     steps = rows // local_reqs
     block_width = channels // splits
     chunk = scan_chunk_of(block_width)
     chunks = block_width // chunk
+    tiles = chunk // 128
+    loads = bring(
+        load_sem,
+        (conv_out_far, conv_out),
+        (normed_far, normed),
+        (coefs_far, coefs),
+        (place_back_far, place_back),
+        (dt_bias_far, dt_bias),
+        (a_log_far, a_log),
+        (skip_d_far, skip_d),
+    )
+
+    def state_copy(tile):
+        lanes = pl.ds(pl.multiple_of(tile * 128, 128), 128)
+        return pltpu.make_async_copy(state.at[:, lanes], held.at[tile], state_sem.at[tile])
+
     for w_at in range(chunks):
         for split in range(splits):
             at = split * chunks + w_at
             cols = pl.ds(at * chunk, chunk)
-            pltpu.make_async_copy(dt_proj.at[:, cols], rate_w.at[:, cols], chunk_sem.at[0, at]).start()
-            pltpu.make_async_copy(
-                state.at[:, :, cols], held.at[:, :, cols], chunk_sem.at[1, at]
-            ).start()
+            pltpu.make_async_copy(dt_proj.at[:, cols], rate_w.at[:, cols], chunk_sem.at[at]).start()
+            for tile in range(tiles):
+                state_copy(at * tiles + tile).start()
     own_o = pltpu.make_async_copy(ob.at[me], o_out.at[me], local_sem.at[0])
     own_o.start()
     greet(("req",))
@@ -346,6 +417,17 @@
         )
         o_copies[-1].start()
 
+    for copy in loads:
+        copy.wait()
+    for t in range(steps):
+        at_rows = slice(t * local_reqs, (t + 1) * local_reqs)
+        for entry in range(state_size):
+            for wide, column in ((b_wide, entry), (c_wide, state_size + entry)):
+                wide[t, entry] = jnp.broadcast_to(
+                    coefs[at_rows, column : column + 1], (local_reqs, 128)
+                )
+    groups = local_reqs // 8
+
     def one_chunk(w_at, carry):
         inner = pl.ds(pl.multiple_of(w_at * chunk, chunk), chunk)
         blocks = jnp.zeros((n * BLOCK_ROWS, chunk), jnp.float32)
@@ -353,7 +435,7 @@
             at = split * chunks + w_at
             outer = pl.ds(pl.multiple_of(at * chunk, chunk), chunk)
             pltpu.make_async_copy(
-                dt_proj.at[:, outer], rate_w.at[:, outer], chunk_sem.at[0, at]
+                dt_proj.at[:, outer], rate_w.at[:, outer], chunk_sem.at[at]
             ).wait()
             raw = (
                 jnp.dot(normed[...], rate_w[:, outer], preferred_element_type=jnp.float32)
@@ -363,23 +445,34 @@
             inputs = conv_out[:, outer].astype(jnp.float32)
             rates[...] = rate
             drives[...] = rate * inputs
-            decay = jnp.exp(a_log[:, outer]) * (-LOG2E)
-            pltpu.make_async_copy(
-                state.at[:, :, outer], held.at[:, :, outer], chunk_sem.at[1, at]
-            ).wait()
-
-            def one_request(req, inner_carry):
-                hidden = held[req, :, outer]
-                pair = coefs[req]
+            decay[...] = jnp.exp(a_log[:, outer]) * (-LOG2E)
+            for tile in range(tiles):
+                state_copy(at * tiles + tile).wait()
+
+            def one_tile(cell, inner_carry):
+                tile = cell // groups
+                first = pl.multiple_of((cell - tile * groups) * 8, 8)
+                lanes = pl.ds(pl.multiple_of(tile * 128, 128), 128)
+                rows_at = [pl.ds(pl.multiple_of(t * local_reqs + first, 8), 8) for t in range(steps)]
+                rate_t = [rates[rows_at[t], lanes] for t in range(steps)]
+                drive_t = [drives[rows_at[t], lanes] for t in range(steps)]
+                sums = [jnp.zeros((8, 128), jnp.float32) for _ in range(steps)]
+                for entry in range(state_size):
+                    hidden = held[
+                        at * tiles + tile, pl.ds(first * state_size + entry, 8, stride=state_size), :
+                    ]
+                    slope = decay[entry : entry + 1, lanes]
+                    for t in range(steps):
+                        hidden = (
+                            jnp.exp2(rate_t[t] * slope) * hidden
+                            + drive_t[t] * b_wide[t, entry, pl.ds(first, 8), :]
+                        )
+                        sums[t] = sums[t] + hidden * c_wide[t, entry, pl.ds(first, 8), :]
                 for t in range(steps):
-                    row = pl.ds(t * local_reqs + req, 1)
-                    hidden = jnp.exp2(rates[row, :] * decay) * hidden + drives[row, :] * pair[:, t : t + 1]
-                    readings[row, :] = jnp.sum(
-                        hidden * pair[:, steps + t : steps + t + 1], axis=0, keepdims=True
-                    )
+                    readings[rows_at[t], lanes] = sums[t]
                 return inner_carry
 
-            lax.fori_loop(0, local_reqs, one_request, 0)
+            lax.fori_loop(0, tiles * groups, one_tile, 0)
             reading = (readings[...] + skip_d[:, outer] * inputs).astype(jnp.bfloat16)
             blocks = blocks + jnp.dot(
                 place_back[split], reading, preferred_element_type=jnp.float32
@@ -414,7 +507,10 @@
 def back(ob, conv_out, normed, coefs, place_back, dt_proj, dt_bias, a_log, skip_d, state):
     n = ob.shape[0]
     splits, block_total, rows = place_back.shape
-    channels = state.shape[2]
+    channels = state.shape[1]
+    state_size = a_log.shape[0]
+    local_reqs = state.shape[0] // state_size
+    steps = rows // local_reqs
     block_width = channels // splits
     chunk = scan_chunk_of(block_width)
     dma = pltpu.SemaphoreType.DMA
@@ -425,10 +521,21 @@
             jax.ShapeDtypeStruct(ob.shape, ob.dtype),
             jax.ShapeDtypeStruct(blocks, jnp.bfloat16),
         ),
-        in_specs=[ANY, VMEM, VMEM, VMEM, VMEM, ANY, VMEM, VMEM, VMEM, ANY],
+        in_specs=[ANY] * 10,
         out_specs=(ANY, ANY),
         scratch_shapes=[
-            pltpu.VMEM(state.shape, state.dtype),
+            like(conv_out),
+            like(normed),
+            like(coefs),
+            like(place_back),
+            like(dt_bias),
+            like(a_log),
+            like(skip_d),
+            dma((7,)),
+            pltpu.VMEM((steps, state_size, local_reqs, 128), jnp.float32),
+            pltpu.VMEM((steps, state_size, local_reqs, 128), jnp.float32),
+            pltpu.VMEM((state_size, chunk), jnp.float32),
+            pltpu.VMEM((channels // 128, local_reqs * state_size, 128), jnp.float32),
             pltpu.VMEM(dt_proj.shape, dt_proj.dtype),
             pltpu.VMEM((rows, chunk), jnp.float32),
             pltpu.VMEM((rows, chunk), jnp.float32),
@@ -439,7 +546,8 @@
             dma((n,)),
             dma((n,)),
             dma((2,)),
-            dma((2, channels // chunk)),
+            dma((channels // chunk,)),
+            dma((channels // 128,)),
         ],
         compiler_params=pltpu.CompilerParams(
             collective_id=1, has_side_effects=True, vmem_limit_bytes=VMEM_LIMIT
@@ -512,7 +620,7 @@
         place,
         conv_weight,
         conv_bias[None],
-        x_proj,
+        x_proj.T,
         dt_gain[None],
     )
     ob = attention(
@@ -525,9 +633,6 @@
         q_rows,
         steps,
     )
-    coefs = jnp.transpose(
-        coefs[:, : 2 * state_size].reshape(steps, local_reqs, 2, state_size), (1, 3, 2, 0)
-    ).reshape(local_reqs, state_size, 2 * steps)
     o_back, y_back = back(
         ob.reshape(n, share * kv_heads * q_rows, HEAD_SIZE),
         conv_out,
@@ -538,7 +643,7 @@
         dt_bias[None],
         a_log,
         skip_d[None],
-        ssm_state,
+        ssm_state.reshape(local_reqs * state_size, channels),
     )
     attn_out = jnp.transpose(
         o_back.reshape(local_reqs, kv_heads, steps, group_width, HEAD_SIZE), (2, 0, 1, 3, 4)

time: 152 us -> 116 us (0.76)
  Pallas kernels: 119 us -> 97.1 us
  local copies, waits for them, and re-layouts: 27 us -> 12.6 us
    pallas_call x1, Pallas kernels: 28 us -> 7.35 us  [attention(): pl.pallas_call(functools.partial(attention_kernel, kv_heads, q_rows, step...]
    unnamed x47 -> x8, local copies, waits for them, and re-layouts: 19.3 us -> 2.52 us
    pallas_call x1, Pallas kernels: 50.4 us -> 44.5 us  [back(): pl.pallas_call(back_kernel, out_shape=(jax.ShapeDtypeStruct(ob.shape, ob....]
    pallas_call x1, Pallas kernels: 40.2 us -> 45.3 us  [front(): pl.pallas_call(front_kernel, out_shape=(jax.ShapeDtypeStruct((rows, chann...]
where the time goes in v3:
time: 116 us
  Pallas kernels  97.1 us (84%)
  local copies, waits for them, and re-layouts  12.6 us (11%)
  other arithmetic  5.36 us (5%)
    pallas_call x1, Pallas kernels, front(): pl.pallas_call(front_kernel, out_shape=(jax.ShapeDtypeStruct((rows, chann...  45.3 us
    pallas_call x1, Pallas kernels, back(): pl.pallas_call(back_kernel, out_shape=(jax.ShapeDtypeStruct(ob.shape, ob....  44.5 us
    pallas_call x1, Pallas kernels, attention(): pl.pallas_call(functools.partial(attention_kernel, kv_heads, q_rows, step...  7.35 us
    convert_element_type x3, local copies, waits for them, and re-layouts, per_device(): mamba_out = (reading.astype(jnp.float32) * gate_values).astype(jnp.bfloat16)  4.21 us
    unnamed x8, local copies, waits for them, and re-layouts  2.52 us

profile of v3, /device:TPU:0, one launch (start us, length us, event | category | flops | bytes accessed | tf_op | source)
XLA Modules:
  0.0 115.9 jit_solution(14173887316996985400)
XLA Ops:
  0.6 0.9 convert_reduce_fusion
  1.6 1.2 %multiply_add_fusion = (s32[32]{0:T(128)S(1)}, s32[32]{0:T(128)}) fusion(s32[32]{0:T(128)S(1)} %convert_reduce_fusion, s32[32]{0:T(128)} %param.23), kind=kLoop, calls=%fused_computation.17 | loop fusion | flops 128 | bytes 512 | tf_op jit(solution)/shard_map/add | solution.py:595
  2.8 0.1 add.40
  2.9 0.1 add.41
  3.0 0.1 add.42
  3.1 1.4 %copy.29.table = s32[32,8]{1,0:T(8,128)} copy(s32[32,8]{0,1:T(8,128)} %param.21) | data formatting | bytes 2048 | tf_op args[3]
  4.4 0.7 fusion.6
  5.1 1.0 reshape.167
  6.1 0.2 copy.28
  6.3 1.1 copy.32
  7.5 0.1 copy.27
  7.6 0.9 pad_maximum_fusion
  8.5 0.4 reshape.163
  8.9 0.6 copy.34
  9.6 1.1 reshape.164.xb
  10.7 45.3 %shard_map.185 = (bf16[128,4096]{1,0:T(8,128)(2,1)}, bf16[128,512]{1,0:T(8,128)(2,1)}, f32[128,128]{1,0:T(8,128)}, bf16[8,320,128]{2,1,0:T(8,128)(2,1)}) custom-call(bf16[8,16,4096]{2,1,0:T(8,128)(2,1)} %reshape.164.xb, bf16[8,320,128]{2,1,0:T(8,128)(2,1)} %bitcast.34, bf16[3,32,4096]{2,1,0:T(8,128)(2,1)} %bitcast.38, ...), custom_call_target="tpu_custom_call" | custom-call | tf_op jit(solution)/shard_map/pallas_call | solution.py:214
  56.0 7.3 %shard_map.186 = bf16[32,64,128]{2,1,0:T(8,128)(2,1)} custom-call(s32[32,8]{1,0:T(8,128)} %copy.29.table, s32[32]{0:T(128)} %lengths.1, s32[32]{0:T(128)} %get-tuple-element.15.slots, bf16[32,80,128]{2,1,0:T(8,128)(2,1)} %bitcast.39, bf16[256,2,16,256]{3,2,1,0:T(8,128)(2,1)} %pool.1), custom_call_target="tpu_custom_call" | custom-call | tf_op jit(solution)/shard_map/pallas_call | solution.py:326
  63.3 44.5 %shard_map.187 = (bf16[8,256,128]{2,1,0:T(8,128)(2,1)}, bf16[8,16,4096]{2,1,0:T(8,128)(2,1)}) custom-call(bf16[8,256,128]{2,1,0:T(8,128)(2,1)} %bitcast.35, bf16[128,4096]{1,0:T(8,128)(2,1)} %get-tuple-element.9.conv_out_far, bf16[128,512]{1,0:T(8,128)(2,1)} %get-tuple-element.10.normed_far, f32[128,128]{1,0:T(8,128)} %get-tuple-element.11.coefs_far, ...), custom_call_target="tpu_custom_call" | custom-call | tf_op jit(solution)/shard_map/pallas_call | solution.py:518
  107.8 1.2 %copy.30 = bf16[4,32,2,8,128]{4,3,2,1,0:T(8,128)(2,1)S(1)} copy(bf16[4,32,2,8,128]{4,3,0,2,1:T(8,128)(2,1)} %bitcast.42) | data formatting | bytes 1048576 | tf_op jit(solution)/shard_map/transpose | solution.py:648
  109.1 1.0 reshape.174
  110.1 0.7 reshape.176
  110.8 1.5 %copy.31 = f32[4,8,4,4096]{3,2,1,0:T(4,128)} copy(f32[4,8,4,4096]{3,2,0,1:T(4,128)S(1)} %bitcast.31) | data formatting | bytes 4194304 | tf_op jit(solution)/shard_map/convert_element_type | solution.py:655
  112.3 2.1 %reshape.175 = f32[4,32,4096]{2,1,0:T(8,128)S(1)} reshape(f32[4,8,4,4096]{3,2,1,0:T(4,128)} %copy.31) | data formatting | bytes 4194304 | tf_op jit(solution)/shard_map/convert_element_type | solution.py:655
  114.3 1.6 %fusion.4 = bf16[4,32,4096]{2,1,0:T(8,128)(2,1)} fusion(f32[4,32,4096]{2,1,0:T(8,128)S(1)} %reshape.175, bf16[4,32,4096]{2,1,0:T(8,128)(2,1)S(1)} %copy-done.2), kind=kLoop, calls=%fused_computation.6 | loop fusion | flops 3670016 | bytes 4194304 | tf_op jit(solution)/shard_map/convert_element_type | solution.py:655
  (9 shorter events, 0.0 us)
Async XLA Ops:
  0.6 7.9 %copy-start.1 = (bf16[4,32,4096]{2,1,0:T(8,128)(2,1)S(1)}, bf16[4,32,4096]{2,1,0:T(8,128)(2,1)}, u32[]{:S(2)}) copy-start(bf16[4,32,4096]{2,1,0:T(8,128)(2,1)} %param.26) | copy-start | bytes 3145732
  107.8 2.3 %copy-start = (bf16[8,16,4096]{2,1,0:T(8,128)(2,1)S(1)}, bf16[8,16,4096]{2,1,0:T(8,128)(2,1)}, u32[]{:S(2)}) copy-start(bf16[8,16,4096]{2,1,0:T(8,128)(2,1)} %get-tuple-element.13) | copy-start | bytes 3145732
  112.3 2.1 %copy-start.2 = (bf16[4,32,4096]{2,1,0:T(8,128)(2,1)S(1)}, bf16[4,32,4096]{2,1,0:T(8,128)(2,1)}, u32[]{:S(2)}) copy-start(bf16[4,32,4096]{2,1,0:T(8,128)(2,1)} %param.27) | copy-start | bytes 3145732

commit v4 on v3

v4 whole, which is shorter than its diff:
```python
import functools
import math

import jax
import jax.numpy as jnp
from jax import lax
from jax.experimental import pallas as pl
from jax.experimental.pallas import tpu as pltpu
from jax.sharding import PartitionSpec as P

HEAD_SIZE = 128
BLOCK_ROWS = 16
X_PARTS = 2
EPSILON = 1e-06
LOG2E = 1.4426950408889634
VMEM_LIMIT = 56 * 1024 * 1024
MESH = pl.DeviceIdType.MESH
ANY = pl.BlockSpec(memory_space=pl.ANY)
VMEM = pl.BlockSpec(memory_space=pltpu.VMEM)


def greet(axes):
    barrier = pltpu.get_barrier_semaphore()
    total = 0
    for name in axes:
        size = lax.axis_size(name)
        me = lax.axis_index(name)
        for step in range(1, size):
            pl.semaphore_signal(
                barrier, inc=1, device_id={name: lax.rem(me + step, size)}, device_id_type=MESH
            )
        total += size - 1
    pl.semaphore_wait(barrier, total)


def remote(src, dst, send_sem, recv_sem, axis, peer):
    return pltpu.make_async_remote_copy(
        src_ref=src,
        dst_ref=dst,
        send_sem=send_sem,
        recv_sem=recv_sem,
        device_id={axis: peer},
        device_id_type=MESH,
    )


def bring(sems, *pairs):
    copies = [
        pltpu.make_async_copy(src, dst, sems.at[at]) for at, (src, dst) in enumerate(pairs)
    ]
    for copy in copies:
        copy.start()
    return copies


def like(value):
    return pltpu.VMEM(value.shape, value.dtype)


def decode_kernel(
    kv_heads,
    q_rows,
    steps,
    table,
    lengths,
    order,
    qb,
    xb,
    pool_far,
    conv_rows_far,
    place_far,
    place_back_far,
    conv_weight_far,
    conv_bias_far,
    x_proj,
    dt_gain_far,
    dt_proj,
    dt_bias_far,
    a_log_far,
    skip_d_far,
    state,
    o_out,
    y_out,
    pool,
    conv_rows,
    place,
    place_back,
    conv_weight,
    conv_bias,
    dt_gain,
    dt_bias,
    a_log,
    skip_d,
    proj_w,
    load_sem,
    q_in,
    x_in,
    o_ready,
    conv_out,
    part,
    gathered,
    normed,
    coefs,
    b_wide,
    c_wide,
    decay,
    held,
    rate_w,
    rates,
    drives,
    readings,
    ready,
    q_send,
    q_recv,
    x_send,
    x_recv,
    o_send,
    o_recv,
    y_send,
    y_recv,
    local_sem,
    chunk_sem,
    state_sem,
    rs_send,
    rs_recv,
    ag_send,
    ag_recv,
):
    n = lax.axis_size("req")
    width = lax.axis_size("tp")
    me = lax.axis_index("req")
    lane = lax.axis_index("tp")
    splits, rows, _ = place.shape
    block_width = xb.shape[2]
    local_reqs, list_len = table.shape
    share = local_reqs // n
    state_size, channels = a_log.shape
    taps = conv_weight.shape[0]
    rank_width = dt_gain.shape[1]
    proj_width = x_proj.shape[0]
    piece = rows // width
    half = block_width // X_PARTS
    chunk = min(512, half)
    span = scan_chunk_of(block_width)
    chunks = block_width // span
    spans = chunks
    tiles = span // 128
    mine_rows = pl.ds(me * share, share)
    own_q = pltpu.make_async_copy(qb.at[mine_rows], q_in.at[mine_rows], local_sem.at[0])
    own_q.start()
    own_x = pltpu.make_async_copy(xb.at[me], x_in.at[me], local_sem.at[1])
    own_x.start()
    loads = bring(
        load_sem,
        (pool_far, pool),
        (x_proj, proj_w),
        (conv_rows_far, conv_rows),
        (place_far, place),
        (place_back_far, place_back),
        (conv_weight_far, conv_weight),
        (conv_bias_far, conv_bias),
        (dt_gain_far, dt_gain),
        (dt_bias_far, dt_bias),
        (a_log_far, a_log),
        (skip_d_far, skip_d),
    )
    greet(("req", "tp"))
    peers = [lax.rem(me + step, n) for step in range(1, n)]
    q_copies, x_copies, o_copies = [], [], []
    for at, peer in enumerate(peers):
        q_copies.append(
            remote(
                qb.at[pl.ds(peer * share, share)],
                q_in.at[mine_rows],
                q_send.at[at],
                q_recv.at[at],
                "req",
                peer,
            )
        )
        q_copies[-1].start()
        o_copies.append(
            remote(
                o_ready.at[pl.ds(peer * share, share)],
                o_out.at[mine_rows],
                o_send.at[at],
                o_recv.at[at],
                "req",
                peer,
            )
        )
    for copy in q_copies:
        copy.wait_send()
    for portion in range(X_PARTS):
        cols = slice(portion * half, (portion + 1) * half)
        x_copies.append([])
        for at, peer in enumerate(peers):
            x_copies[-1].append(
                remote(
                    xb.at[peer, :, cols],
                    x_in.at[me, :, cols],
                    x_send.at[portion, at],
                    x_recv.at[portion, at],
                    "req",
                    peer,
                )
            )
            x_copies[-1][-1].start()

    def state_copy(tile):
        lanes = pl.ds(pl.multiple_of(tile * 128, 128), 128)
        return pltpu.make_async_copy(state.at[:, lanes], held.at[tile], state_sem.at[tile])

    for w_at in range(chunks):
        for split in range(splits):
            at = split * chunks + w_at
            cols = pl.ds(at * span, span)
            pltpu.make_async_copy(dt_proj.at[:, cols], rate_w.at[:, cols], chunk_sem.at[at]).start()
            for tile in range(tiles):
                state_copy(at * tiles + tile).start()
    part[...] = jnp.zeros_like(part)
    for copy in loads:
        copy.wait()
    own_q.wait()
    for copy in q_copies:
        copy.wait_recv()

    cache_len = list_len * pool.shape[2]
    scale = 1.0 / math.sqrt(HEAD_SIZE)
    recent = kv_heads * steps
    all_rows = kv_heads * q_rows
    group_width = q_rows // steps
    token = lax.broadcasted_iota(jnp.int32, (all_rows, cache_len), 1)
    column = lax.broadcasted_iota(jnp.int32, (all_rows, recent), 1)
    row = lax.broadcasted_iota(jnp.int32, (all_rows, recent), 0)
    row_head = row // q_rows
    row_moment = (row - row_head * q_rows) // group_width
    seen = (column >= row_head * steps) & (column <= row_head * steps + row_moment)
    contract = (((1,), (1,)), ((), ()))
    together = 4

    def some_requests(at, carry):
        reqs = [at * together + offset for offset in range(together)]
        rows = reqs
        reqs = [order[slot] for slot in rows]
        scores, fresh = [], []
        for req, slot in zip(reqs, rows):
            keys = jnp.concatenate([pool[table[req, i], 0] for i in range(list_len)], axis=0)
            parts = [
                lax.dot_general(
                    q_in[slot, head * q_rows : (head + 1) * q_rows, :],
                    keys[:, head * HEAD_SIZE : (head + 1) * HEAD_SIZE],
                    contract,
                    preferred_element_type=jnp.float32,
                )
                for head in range(kv_heads)
            ]
            scores.append(jnp.concatenate(parts, axis=0))
            fresh.append(
                lax.dot_general(
                    q_in[slot, :all_rows, :],
                    q_in[slot, all_rows : all_rows + recent, :],
                    contract,
                    preferred_element_type=jnp.float32,
                )
            )
        weights = []
        for req, old, new in zip(reqs, scores, fresh):
            old = jnp.where(token < lengths[req], old * scale, -jnp.inf)
            new = jnp.where(seen, new * scale, -jnp.inf)
            top = jnp.maximum(
                jnp.max(old, axis=1, keepdims=True), jnp.max(new, axis=1, keepdims=True)
            )
            old = jnp.exp(old - top)
            new = jnp.exp(new - top)
            total = jnp.sum(old, axis=1, keepdims=True) + jnp.sum(new, axis=1, keepdims=True)
            weights.append((old.astype(jnp.bfloat16), new.astype(jnp.bfloat16), 1.0 / total))
        for req, slot, (old, new, inverse) in zip(reqs, rows, weights):
            values = jnp.concatenate([pool[table[req, i], 1] for i in range(list_len)], axis=0)
            parts = [
                jnp.dot(
                    old[head * q_rows : (head + 1) * q_rows, :],
                    values[:, head * HEAD_SIZE : (head + 1) * HEAD_SIZE],
                    preferred_element_type=jnp.float32,
                )
                for head in range(kv_heads)
            ]
            mixed = jnp.concatenate(parts, axis=0) + jnp.dot(
                new,
                q_in[slot, all_rows + recent : all_rows + 2 * recent, :],
                preferred_element_type=jnp.float32,
            )
            o_ready[slot] = (mixed * inverse).astype(jnp.bfloat16)
        return carry

    lax.fori_loop(0, local_reqs // together, some_requests, 0)

    own_x.wait()
    for portion in range(X_PARTS):
        for copy in x_copies[portion]:
            copy.wait_recv()
        for split in range(splits):

            def conv_chunk(at, carry):
                inner = pl.ds(pl.multiple_of(at * chunk, chunk), chunk)
                outer = pl.ds(pl.multiple_of(split * block_width + at * chunk, chunk), chunk)
                block = x_in[:, :, inner].reshape(n * BLOCK_ROWS, chunk)
                fresh = jnp.dot(place[split], block, preferred_element_type=jnp.float32)
                window = [conv_rows[row, :, outer].astype(jnp.float32) for row in range(taps - 1)]
                window += [fresh[t * local_reqs : (t + 1) * local_reqs] for t in range(steps)]
                for t in range(steps):
                    total = conv_bias[:, outer] + sum(
                        conv_weight[tap : tap + 1, outer] * window[t + tap] for tap in range(taps)
                    )
                    active = total / (1.0 + jnp.exp(-total))
                    conv_out[t * local_reqs : (t + 1) * local_reqs, outer] = active.astype(jnp.bfloat16)
                part[:, :proj_width] += lax.dot_general(
                    conv_out[:, outer],
                    proj_w[:, outer],
                    (((1,), (1,)), ((), ())),
                    preferred_element_type=jnp.float32,
                )
                return carry

            lax.fori_loop(
                portion * (half // chunk), (portion + 1) * (half // chunk), conv_chunk, 0
            )
        if portion == 0:
            for copies in x_copies:
                for copy in copies:
                    copy.wait_send()
            for copy in o_copies:
                copy.start()
            own_o = pltpu.make_async_copy(
                o_ready.at[mine_rows], o_out.at[mine_rows], local_sem.at[2]
            )
            own_o.start()
    copies = []
    for step in range(1, width):
        peer = lax.rem(lane + step, width)
        copies.append(
            remote(
                part.at[pl.ds(pl.multiple_of(peer * piece, piece), piece)],
                gathered.at[step],
                rs_send.at[step],
                rs_recv.at[step],
                "tp",
                peer,
            )
        )
        copies[-1].start()
    mine = pl.ds(pl.multiple_of(lane * piece, piece), piece)
    gathered[0] = part[mine, :]
    for copy in copies:
        copy.wait()
    summed = gathered[0]
    for step in range(1, width):
        summed = summed + gathered[step]
    dt_low = summed[:, :rank_width]
    scale = lax.rsqrt(jnp.mean(dt_low * dt_low, axis=-1, keepdims=True) + EPSILON)
    normed[mine, :] = (dt_low * scale * dt_gain[...]).astype(jnp.bfloat16)
    coefs[mine, :] = summed[:, rank_width:]
    copies = []
    for step in range(1, width):
        peer = lax.rem(lane + step, width)
        for at, ref in enumerate((normed, coefs)):
            copies.append(
                remote(
                    ref.at[mine], ref.at[mine], ag_send.at[at, step], ag_recv.at[at, step], "tp", peer
                )
            )
            copies[-1].start()
    for copy in copies:
        copy.wait()
    for t in range(steps):
        at_rows = slice(t * local_reqs, (t + 1) * local_reqs)
        for entry in range(state_size):
            for wide, column in ((b_wide, entry), (c_wide, state_size + entry)):
                wide[t, entry] = jnp.broadcast_to(
                    coefs[at_rows, column : column + 1], (local_reqs, 128)
                )
    groups = local_reqs // 8

    def scan_chunk(w_at, carry):
        inner = pl.ds(pl.multiple_of(w_at * span, span), span)
        blocks = jnp.zeros((n * BLOCK_ROWS, span), jnp.float32)
        for split in range(splits):
            at = split * spans + w_at
            outer = pl.ds(pl.multiple_of(at * span, span), span)
            pltpu.make_async_copy(
                dt_proj.at[:, outer], rate_w.at[:, outer], chunk_sem.at[at]
            ).wait()
            raw = (
                jnp.dot(normed[...], rate_w[:, outer], preferred_element_type=jnp.float32)
                + dt_bias[:, outer]
            )
            rate = jnp.maximum(raw, 0.0) + jnp.log1p(jnp.exp(-jnp.abs(raw)))
            inputs = conv_out[:, outer].astype(jnp.float32)
            rates[...] = rate
            drives[...] = rate * inputs
            decay[...] = jnp.exp(a_log[:, outer]) * (-LOG2E)
            for tile in range(tiles):
                state_copy(at * tiles + tile).wait()

            def one_tile(cell, inner_carry):
                tile = cell // groups
                first = pl.multiple_of((cell - tile * groups) * 8, 8)
                lanes = pl.ds(pl.multiple_of(tile * 128, 128), 128)
                rows_at = [pl.ds(pl.multiple_of(t * local_reqs + first, 8), 8) for t in range(steps)]
                rate_t = [rates[rows_at[t], lanes] for t in range(steps)]
                drive_t = [drives[rows_at[t], lanes] for t in range(steps)]
                sums = [jnp.zeros((8, 128), jnp.float32) for _ in range(steps)]
                for entry in range(state_size):
                    hidden = held[
                        at * tiles + tile, pl.ds(first * state_size + entry, 8, stride=state_size), :
                    ]
                    slope = decay[entry : entry + 1, lanes]
                    for t in range(steps):
                        hidden = (
                            jnp.exp2(rate_t[t] * slope) * hidden
                            + drive_t[t] * b_wide[t, entry, pl.ds(first, 8), :]
                        )
                        sums[t] = sums[t] + hidden * c_wide[t, entry, pl.ds(first, 8), :]
                for t in range(steps):
                    readings[rows_at[t], lanes] = sums[t]
                return inner_carry

            lax.fori_loop(0, tiles * groups, one_tile, 0)
            reading = (readings[...] + skip_d[:, outer] * inputs).astype(jnp.bfloat16)
            blocks = blocks + jnp.dot(
                place_back[split], reading, preferred_element_type=jnp.float32
            )
        ready[:, :, inner] = blocks.astype(jnp.bfloat16).reshape(n, BLOCK_ROWS, span)
        for step in range(1, n):
            peer = lax.rem(me + step, n)
            remote(
                ready.at[peer, :, inner],
                y_out.at[me, :, inner],
                y_send.at[step],
                y_recv.at[step],
                "req",
                peer,
            ).start()
        return carry

    lax.fori_loop(0, chunks, scan_chunk, 0)
    own_y = pltpu.make_async_copy(ready.at[me], y_out.at[me], local_sem.at[3])
    own_y.start()
    own_o.wait()
    for copy in o_copies:
        copy.wait()
    for step in range(1, n):
        peer = lax.rem(me + step, n)
        remote(
            ready.at[peer], y_out.at[me], y_send.at[step], y_recv.at[step], "req", peer
        ).wait()
    own_y.wait()


def scan_chunk_of(block_width):
    return min(512, block_width)


def decode(
    table,
    lengths,
    order,
    qb,
    xb,
    pool,
    conv_rows,
    place,
    place_back,
    conv_weight,
    conv_bias,
    x_proj,
    dt_gain,
    dt_proj,
    dt_bias,
    a_log,
    skip_d,
    state,
    kv_heads,
    q_rows,
    steps,
):
    n = xb.shape[0]
    width = lax.axis_size("tp")
    local_reqs = table.shape[0]
    rows = place.shape[1]
    state_size, channels = a_log.shape
    rank_width = dt_gain.shape[1]
    wide = rank_width + 128
    span = scan_chunk_of(xb.shape[2])
    dma = pltpu.SemaphoreType.DMA
    smem = pl.BlockSpec(memory_space=pltpu.SMEM)
    outs = jax.ShapeDtypeStruct((local_reqs, kv_heads * q_rows, HEAD_SIZE), jnp.bfloat16)
    return pl.pallas_call(
        functools.partial(decode_kernel, kv_heads, q_rows, steps),
        out_shape=(outs, jax.ShapeDtypeStruct(xb.shape, jnp.bfloat16)),
        in_specs=[smem] * 3 + [ANY] * 15,
        out_specs=(ANY, ANY),
        scratch_shapes=[
            like(pool),
            like(conv_rows),
            like(place),
            like(place_back),
            like(conv_weight),
            like(conv_bias),
            like(dt_gain),
            like(dt_bias),
            like(a_log),
            like(skip_d),
            like(x_proj),
            dma((11,)),
            like(qb),
            like(xb),
            like(outs),
            pltpu.VMEM((rows, channels), jnp.bfloat16),
            pltpu.VMEM((rows, wide), jnp.float32),
            pltpu.VMEM((width, rows // width, wide), jnp.float32),
            pltpu.VMEM((rows, rank_width), jnp.bfloat16),
            pltpu.VMEM((rows, 128), jnp.float32),
            pltpu.VMEM((steps, state_size, local_reqs, 128), jnp.float32),
            pltpu.VMEM((steps, state_size, local_reqs, 128), jnp.float32),
            pltpu.VMEM((state_size, span), jnp.float32),
            pltpu.VMEM((channels // 128, local_reqs * state_size, 128), jnp.float32),
            like(dt_proj),
            pltpu.VMEM((rows, span), jnp.float32),
            pltpu.VMEM((rows, span), jnp.float32),
            pltpu.VMEM((rows, span), jnp.float32),
            like(xb),
            dma((n,)),
            dma((n,)),
            dma((X_PARTS, n)),
            dma((X_PARTS, n)),
            dma((n,)),
            dma((n,)),
            dma((n,)),
            dma((n,)),
            dma((4,)),
            dma((channels // span,)),
            dma((channels // 128,)),
            dma((width,)),
            dma((width,)),
            dma((2, width)),
            dma((2, width)),
        ],
        compiler_params=pltpu.CompilerParams(
            collective_id=0, has_side_effects=True, vmem_limit_bytes=VMEM_LIMIT
        ),
    )(
        table,
        lengths,
        order,
        qb,
        xb,
        pool,
        conv_rows,
        place,
        place_back,
        conv_weight,
        conv_bias,
        x_proj,
        dt_gain,
        dt_proj,
        dt_bias,
        a_log,
        skip_d,
        state,
    )


def per_device(
    queries,
    new_kv,
    prefill_page_pool,
    page_table,
    prompt_len,
    dest_device,
    ssm_state,
    conv_state,
    mamba_x,
    mamba_z,
    conv_weight,
    conv_bias,
    x_proj,
    dt_gain,
    dt_proj,
    dt_bias,
    a_log,
    skip_d,
):
    n = lax.axis_size("req")
    local_reqs = dest_device.shape[0]
    steps = queries.shape[0]
    channels = mamba_x.shape[2]
    kv_heads = prefill_page_pool.shape[3] // HEAD_SIZE
    group_width = queries.shape[2] // HEAD_SIZE // kv_heads
    q_rows = steps * group_width
    state_size = a_log.shape[0]
    share = local_reqs // n
    splits = BLOCK_ROWS // (steps * share)
    block_width = channels // splits
    index = jnp.arange(local_reqs, dtype=jnp.int32)
    same = dest_device[:, None] == dest_device[None, :]
    rank = jnp.sum((same & (index[None, :] < index[:, None])).astype(jnp.int32), axis=1)
    slots = dest_device * share + rank
    order = jnp.sum(jnp.where(slots[:, None] == index[None, :], index[:, None], 0), axis=0)
    times = jnp.arange(steps, dtype=jnp.int32)
    split_ids = jnp.arange(splits, dtype=jnp.int32)
    block_row = dest_device * BLOCK_ROWS + rank * splits
    block_row = (
        block_row[None, None, :]
        + times[None, :, None] * (share * splits)
        + split_ids[:, None, None]
    ).reshape(splits, steps * local_reqs)
    block_ids = jnp.arange(n * BLOCK_ROWS, dtype=jnp.int32)
    place = (block_row[:, :, None] == block_ids[None, None, :]).astype(jnp.bfloat16)
    place_back = (block_row[:, None, :] == block_ids[None, :, None]).astype(jnp.bfloat16)

    xb = jnp.transpose(
        mamba_x.reshape(steps, n, share, channels), (1, 0, 2, 3)
    ).reshape(n, BLOCK_ROWS, block_width)
    q_part = jnp.transpose(
        queries.reshape(steps, local_reqs, kv_heads, group_width, HEAD_SIZE), (1, 2, 0, 3, 4)
    ).reshape(local_reqs, kv_heads * q_rows, HEAD_SIZE)
    kv_part = jnp.transpose(
        new_kv.reshape(steps, local_reqs, 2, kv_heads, HEAD_SIZE), (1, 2, 3, 0, 4)
    ).reshape(local_reqs, 2 * kv_heads * steps, HEAD_SIZE)
    slabs = jnp.concatenate([q_part, kv_part], axis=1)
    o_back, y_back = decode(
        page_table,
        prompt_len,
        order,
        slabs,
        xb,
        prefill_page_pool,
        jnp.transpose(conv_state, (1, 0, 2)),
        place,
        place_back,
        conv_weight,
        conv_bias[None],
        x_proj.T,
        dt_gain[None],
        dt_proj,
        dt_bias[None],
        a_log,
        skip_d[None],
        ssm_state.reshape(local_reqs * state_size, channels),
        kv_heads,
        q_rows,
        steps,
    )
    attn_out = jnp.transpose(
        o_back.reshape(local_reqs, kv_heads, steps, group_width, HEAD_SIZE), (2, 0, 1, 3, 4)
    ).reshape(queries.shape)
    reading = jnp.transpose(
        y_back.reshape(n, steps, share, channels), (1, 0, 2, 3)
    ).reshape(mamba_x.shape)
    gate_values = jax.nn.silu(mamba_z.astype(jnp.float32))
    mamba_out = (reading.astype(jnp.float32) * gate_values).astype(jnp.bfloat16)
    return (attn_out, mamba_out)


def solution(mesh):
    return jax.shard_map(
        per_device,
        mesh=mesh,
        in_specs=(
            P(None, "req", "tp"),
            P(None, "req", None, "tp"),
            P("req", None, None, "tp"),
            P("req", None),
            P("req"),
            P("req"),
            P("req", None, "tp"),
            P("req", None, "tp"),
            P(None, "req", "tp"),
            P(None, "req", "tp"),
            P(None, "tp"),
            P("tp"),
            P("tp", None),
            P(),
            P(None, "tp"),
            P("tp"),
            P(None, "tp"),
            P("tp"),
        ),
        out_specs=(P(None, "req", "tp"), P(None, "req", "tp")),
        check_vma=False,
    )
```

time: 116 us -> 108 us (0.931)
  Pallas kernels: 97.1 us -> 89.1 us
    pallas_call x3 -> x1, Pallas kernels: 97.1 us -> 89.1 us  [decode(): pl.pallas_call(functools.partial(decode_kernel, kv_heads, q_rows, steps),...]
where the time goes in v4:
time: 108 us
  Pallas kernels  89.1 us (82%)
  local copies, waits for them, and re-layouts  12.7 us (12%)
  other arithmetic  5.44 us (5%)
    pallas_call x1, Pallas kernels, decode(): pl.pallas_call(functools.partial(decode_kernel, kv_heads, q_rows, steps),...  89.1 us
    convert_element_type x3, local copies, waits for them, and re-layouts, per_device(): mamba_out = (reading.astype(jnp.float32) * gate_values).astype(jnp.bfloat16)  4.23 us
    unnamed x8, local copies, waits for them, and re-layouts  2.53 us

profile of v4, /device:TPU:0, one launch (start us, length us, event | category | flops | bytes accessed | tf_op | source)
XLA Modules:
  0.0 107.9 jit_solution(12890723349524068367)
XLA Ops:
  0.6 0.9 convert_reduce_fusion
  1.6 0.7 multiply_add_fusion
  2.2 0.7 select_reduce_fusion.order
  2.9 0.1 add.40
  3.0 0.1 add.41
  3.1 0.1 add.42
  3.2 1.4 %copy.29.table = s32[32,8]{1,0:T(8,128)} copy(s32[32,8]{0,1:T(8,128)} %param.21) | data formatting | bytes 2048 | tf_op args[3]
  4.5 0.7 fusion.6
  5.2 1.0 reshape.157
  6.2 0.2 copy.27
  6.4 1.1 %copy.32 = bf16[16,8,16,128]{3,2,1,0:T(8,128)(2,1)S(1)} copy(bf16[16,8,16,128]{3,1,2,0:T(8,128)(2,1)} %bitcast.36) | data formatting | bytes 1048576
  7.6 0.1 copy.26
  7.7 0.9 pad_maximum_fusion.qb
  8.6 0.4 reshape.159
  9.0 0.6 copy.34
  9.7 1.1 %reshape.160.xb = bf16[8,16,4096]{2,1,0:T(8,128)(2,1)} reshape(bf16[8,4,4,4096]{3,2,1,0:T(4,128)(2,1)S(1)} %bitcast.31) | data formatting | bytes 2097152 | tf_op jit(solution)/shard_map/reshape | solution.py:624
  10.8 89.1 %shard_map.185 = (bf16[32,64,128]{2,1,0:T(8,128)(2,1)}, bf16[8,16,4096]{2,1,0:T(8,128)(2,1)}) custom-call(s32[32,8]{1,0:T(8,128)} %copy.29.table, s32[32]{0:T(128)} %lengths.1, s32[32]{0:T(128)} %select_reduce_fusion.order, bf16[32,80,128]{2,1,0:T(8,128)(2,1)} %pad_maximum_fusion.qb, bf16[8,16,4096]{2,1,0:T(8,128)(2,1)} %reshape.160.xb, ...), custom_call_target="tpu_custom_call" | custom-call | tf_op jit(solution)/shard_map/pallas_call | solution.py:498
  99.9 0.0 copy-start
  99.9 1.2 %copy.30 = bf16[4,32,2,8,128]{4,3,2,1,0:T(8,128)(2,1)S(1)} copy(bf16[4,32,2,8,128]{4,3,0,2,1:T(8,128)(2,1)} %bitcast.37) | data formatting | bytes 1048576 | tf_op jit(solution)/shard_map/transpose | solution.py:655
  101.1 1.0 reshape.163
  102.1 0.7 reshape.165
  102.8 1.5 %copy.31 = f32[4,8,4,4096]{3,2,1,0:T(4,128)} copy(f32[4,8,4,4096]{3,2,0,1:T(4,128)S(1)} %bitcast.29) | data formatting | bytes 4194304 | tf_op jit(solution)/shard_map/convert_element_type | solution.py:662
  104.3 2.1 %reshape.164 = f32[4,32,4096]{2,1,0:T(8,128)S(1)} reshape(f32[4,8,4,4096]{3,2,1,0:T(4,128)} %copy.31) | data formatting | bytes 4194304 | tf_op jit(solution)/shard_map/convert_element_type | solution.py:662
  106.4 1.6 %fusion.4 = bf16[4,32,4096]{2,1,0:T(8,128)(2,1)} fusion(f32[4,32,4096]{2,1,0:T(8,128)S(1)} %reshape.164, bf16[4,32,4096]{2,1,0:T(8,128)(2,1)S(1)} %copy-done.2), kind=kLoop, calls=%fused_computation.6 | loop fusion | flops 3670016 | bytes 4194304 | tf_op jit(solution)/shard_map/convert_element_type | solution.py:662
  (8 shorter events, 0.0 us)
Async XLA Ops:
  0.6 8.0 %copy-start.1 = (bf16[4,32,4096]{2,1,0:T(8,128)(2,1)S(1)}, bf16[4,32,4096]{2,1,0:T(8,128)(2,1)}, u32[]{:S(2)}) copy-start(bf16[4,32,4096]{2,1,0:T(8,128)(2,1)} %param.26) | copy-start | bytes 3145732
  99.9 2.3 %copy-start = (bf16[8,16,4096]{2,1,0:T(8,128)(2,1)S(1)}, bf16[8,16,4096]{2,1,0:T(8,128)(2,1)}, u32[]{:S(2)}) copy-start(bf16[8,16,4096]{2,1,0:T(8,128)(2,1)} %get-tuple-element.5) | copy-start | bytes 3145732
  104.3 2.1 %copy-start.2 = (bf16[4,32,4096]{2,1,0:T(8,128)(2,1)S(1)}, bf16[4,32,4096]{2,1,0:T(8,128)(2,1)}, u32[]{:S(2)}) copy-start(bf16[4,32,4096]{2,1,0:T(8,128)(2,1)} %param.27) | copy-start | bytes 3145732

commit v5 on v4

--- a/solution.py
+++ b/solution.py
@@ -11,6 +11,7 @@
 HEAD_SIZE = 128
 BLOCK_ROWS = 16
 X_PARTS = 2
+TILES_TOGETHER = 2
 EPSILON = 1e-06
 LOG2E = 1.4426950408889634
 VMEM_LIMIT = 56 * 1024 * 1024
@@ -132,7 +133,7 @@
     lane = lax.axis_index("tp")
     splits, rows, _ = place.shape
     block_width = xb.shape[2]
-    local_reqs, list_len = table.shape
+    list_len, local_reqs = table.shape
     share = local_reqs // n
     state_size, channels = a_log.shape
     taps = conv_weight.shape[0]
@@ -245,7 +246,7 @@
         reqs = [order[slot] for slot in rows]
         scores, fresh = [], []
         for req, slot in zip(reqs, rows):
-            keys = jnp.concatenate([pool[table[req, i], 0] for i in range(list_len)], axis=0)
+            keys = jnp.concatenate([pool[table[i, req], 0] for i in range(list_len)], axis=0)
             parts = [
                 lax.dot_general(
                     q_in[slot, head * q_rows : (head + 1) * q_rows, :],
@@ -276,7 +277,7 @@
             total = jnp.sum(old, axis=1, keepdims=True) + jnp.sum(new, axis=1, keepdims=True)
             weights.append((old.astype(jnp.bfloat16), new.astype(jnp.bfloat16), 1.0 / total))
         for req, slot, (old, new, inverse) in zip(reqs, rows, weights):
-            values = jnp.concatenate([pool[table[req, i], 1] for i in range(list_len)], axis=0)
+            values = jnp.concatenate([pool[table[i, req], 1] for i in range(list_len)], axis=0)
             parts = [
                 jnp.dot(
                     old[head * q_rows : (head + 1) * q_rows, :],
@@ -402,30 +403,39 @@
             for tile in range(tiles):
                 state_copy(at * tiles + tile).wait()
 
-            def one_tile(cell, inner_carry):
-                tile = cell // groups
-                first = pl.multiple_of((cell - tile * groups) * 8, 8)
-                lanes = pl.ds(pl.multiple_of(tile * 128, 128), 128)
+            def one_cell(cell, inner_carry):
+                pair = cell // groups
+                first = pl.multiple_of((cell - pair * groups) * 8, 8)
+                subs = range(TILES_TOGETHER)
+                lanes = [
+                    pl.ds(pl.multiple_of((pair * TILES_TOGETHER + sub) * 128, 128), 128)
+                    for sub in subs
+                ]
                 rows_at = [pl.ds(pl.multiple_of(t * local_reqs + first, 8), 8) for t in range(steps)]
-                rate_t = [rates[rows_at[t], lanes] for t in range(steps)]
-                drive_t = [drives[rows_at[t], lanes] for t in range(steps)]
-                sums = [jnp.zeros((8, 128), jnp.float32) for _ in range(steps)]
+                rate_t = [[rates[rows_at[t], lanes[sub]] for sub in subs] for t in range(steps)]
+                drive_t = [[drives[rows_at[t], lanes[sub]] for sub in subs] for t in range(steps)]
+                sums = [[jnp.zeros((8, 128), jnp.float32) for _ in subs] for _ in range(steps)]
                 for entry in range(state_size):
-                    hidden = held[
-                        at * tiles + tile, pl.ds(first * state_size + entry, 8, stride=state_size), :
+                    entry_rows = pl.ds(first * state_size + entry, 8, stride=state_size)
+                    hidden = [
+                        held[at * tiles + pair * TILES_TOGETHER + sub, entry_rows, :] for sub in subs
                     ]
-                    slope = decay[entry : entry + 1, lanes]
+                    slope = [decay[entry : entry + 1, lanes[sub]] for sub in subs]
                     for t in range(steps):
-                        hidden = (
-                            jnp.exp2(rate_t[t] * slope) * hidden
-                            + drive_t[t] * b_wide[t, entry, pl.ds(first, 8), :]
-                        )
-                        sums[t] = sums[t] + hidden * c_wide[t, entry, pl.ds(first, 8), :]
+                        b_now = b_wide[t, entry, pl.ds(first, 8), :]
+                        c_now = c_wide[t, entry, pl.ds(first, 8), :]
+                        for sub in subs:
+                            hidden[sub] = (
+                                jnp.exp2(rate_t[t][sub] * slope[sub]) * hidden[sub]
+                                + drive_t[t][sub] * b_now
+                            )
+                            sums[t][sub] = sums[t][sub] + hidden[sub] * c_now
                 for t in range(steps):
-                    readings[rows_at[t], lanes] = sums[t]
+                    for sub in subs:
+                        readings[rows_at[t], lanes[sub]] = sums[t][sub]
                 return inner_carry
 
-            lax.fori_loop(0, tiles * groups, one_tile, 0)
+            lax.fori_loop(0, tiles // TILES_TOGETHER * groups, one_cell, 0)
             reading = (readings[...] + skip_d[:, outer] * inputs).astype(jnp.bfloat16)
             blocks = blocks + jnp.dot(
                 place_back[split], reading, preferred_element_type=jnp.float32
@@ -486,7 +496,7 @@
 ):
     n = xb.shape[0]
     width = lax.axis_size("tp")
-    local_reqs = table.shape[0]
+    local_reqs = table.shape[1]
     rows = place.shape[1]
     state_size, channels = a_log.shape
     rank_width = dt_gain.shape[1]
@@ -619,8 +629,15 @@
     place = (block_row[:, :, None] == block_ids[None, None, :]).astype(jnp.bfloat16)
     place_back = (block_row[:, None, :] == block_ids[None, :, None]).astype(jnp.bfloat16)
 
-    xb = jnp.transpose(
-        mamba_x.reshape(steps, n, share, channels), (1, 0, 2, 3)
+    decode_row = (
+        index[None, :] // share * BLOCK_ROWS
+        + (times[:, None] * share + index[None, :] % share) * splits
+    ).reshape(1, steps * local_reqs) + split_ids[:, None]
+    home = (decode_row[:, :, None] == block_ids[None, None, :]).astype(jnp.bfloat16)
+    flat_x = mamba_x.reshape(steps * local_reqs, channels)
+    xb = sum(
+        jnp.einsum("pb,pc->bc", home[at], flat_x[:, at * block_width : (at + 1) * block_width])
+        for at in range(splits)
     ).reshape(n, BLOCK_ROWS, block_width)
     q_part = jnp.transpose(
         queries.reshape(steps, local_reqs, kv_heads, group_width, HEAD_SIZE), (1, 2, 0, 3, 4)
@@ -630,7 +647,7 @@
     ).reshape(local_reqs, 2 * kv_heads * steps, HEAD_SIZE)
     slabs = jnp.concatenate([q_part, kv_part], axis=1)
     o_back, y_back = decode(
-        page_table,
+        page_table.T,
         prompt_len,
         order,
         slabs,
@@ -655,11 +672,16 @@
     attn_out = jnp.transpose(
         o_back.reshape(local_reqs, kv_heads, steps, group_width, HEAD_SIZE), (2, 0, 1, 3, 4)
     ).reshape(queries.shape)
-    reading = jnp.transpose(
-        y_back.reshape(n, steps, share, channels), (1, 0, 2, 3)
-    ).reshape(mamba_x.shape)
-    gate_values = jax.nn.silu(mamba_z.astype(jnp.float32))
-    mamba_out = (reading.astype(jnp.float32) * gate_values).astype(jnp.bfloat16)
+    flat_y = y_back.reshape(n * BLOCK_ROWS, block_width)
+    reading = jnp.concatenate(
+        [
+            jnp.einsum("pb,bc->pc", home[at], flat_y, preferred_element_type=jnp.float32)
+            for at in range(splits)
+        ],
+        axis=1,
+    )
+    gate_values = jax.nn.silu(mamba_z.astype(jnp.float32)).reshape(reading.shape)
+    mamba_out = (reading * gate_values).astype(jnp.bfloat16).reshape(mamba_x.shape)
     return (attn_out, mamba_out)
 
 

time: 108 us -> 104 us (0.963)
  local copies, waits for them, and re-layouts: 12.7 us -> 6.91 us
  matrix products: 0 us -> 2.9 us
    convert_element_type x3 -> x0, local copies, waits for them, and re-layouts: 4.23 us -> none  [per_device(): mamba_out = (reading.astype(jnp.float32) * gate_values).astype(jnp.bfloat16)]
    dot_general x0 -> x2, matrix products: none -> 2.9 us  [the longest x1 1.45 us: per_device(): jnp.einsum('pb,pc->bc', home[at], flat_x[:, at * block_width:(at + 1) * b...]
    reshape x3 -> x0, local copies, waits for them, and re-layouts: 2.13 us -> none  [the longest x1 1.11 us: per_device(): xb = jnp.transpose(mamba_x.reshape(steps, n, share, channels), (1, 0, 2,...]
    convert_element_type x1 -> x0, other arithmetic: 1.57 us -> none  [per_device(): mamba_out = (reading.astype(jnp.float32) * gate_values).astype(jnp.bfloat16)]
    unnamed x8 -> x7, local copies, waits for them, and re-layouts: 2.53 us -> 3.04 us
where the time goes in v5:
time: 104 us
  Pallas kernels  88.5 us (85%)
  local copies, waits for them, and re-layouts  6.91 us (7%)
  other arithmetic  4.49 us (4%)
  matrix products  2.9 us (3%)
    pallas_call x1, Pallas kernels, decode(): pl.pallas_call(functools.partial(decode_kernel, kv_heads, q_rows, steps),...  88.5 us
    unnamed x7, local copies, waits for them, and re-layouts  3.04 us

profile of v5, /device:TPU:0, one launch (start us, length us, event | category | flops | bytes accessed | tf_op | source)
XLA Modules:
  0.0 103.5 jit_solution(1291576622366680064)
XLA Ops:
  0.6 0.0 copy-start
  0.6 1.2 %copy-done = bf16[4,32,4096]{2,1,0:T(8,128)(2,1)S(1)} copy-done((bf16[4,32,4096]{2,1,0:T(8,128)(2,1)S(1)}, bf16[4,32,4096]{2,1,0:T(8,128)(2,1)}, u32[]{:S(2)}) %copy-start) | copy-done | bytes 1048600
  1.9 0.9 convert_reduce_fusion
  2.8 0.7 multiply_add_fusion.1
  3.4 0.7 select_reduce_fusion.order
  4.1 0.1 add_add_fusion
  4.2 0.1 add.112
  4.3 0.1 add.116
  4.3 0.1 add.117
  4.4 0.1 add.115
  4.5 0.7 fusion.5
  5.2 1.0 reshape.305
  6.2 0.2 copy.27
  6.4 1.1 %copy.29 = bf16[16,8,16,128]{3,2,1,0:T(8,128)(2,1)S(1)} copy(bf16[16,8,16,128]{3,1,2,0:T(8,128)(2,1)} %bitcast.46) | data formatting | bytes 1048576
  7.6 0.1 copy.26
  7.7 0.9 pad_maximum_fusion.qb
  8.6 1.5 %fusion.8.xb = bf16[8,16,4096]{2,1,0:T(8,128)(2,1)} fusion(bf16[128,4096,1]{1,0,2:T(8,128)(2,1)S(1)} %bitcast.36, s32[8,16]{1,0:T(8,128)S(1)} %multiply_add_fusion, s32[128]{0:T(128)S(1)} %add.112), kind=kOutput, calls=%fused_computation.14 | convolution fusion | flops 134234112 | bytes 2098176 | tf_op jit(solution)/shard_map/pb,pc->bc/dot_general | solution.py:639
  10.1 88.5 %shard_map.185 = (bf16[32,64,128]{2,1,0:T(8,128)(2,1)}, bf16[8,16,4096]{2,1,0:T(8,128)(2,1)}) custom-call(s32[8,32]{1,0:T(8,128)} %bitcast.51, s32[32]{0:T(128)} %lengths.1, s32[32]{0:T(128)} %select_reduce_fusion.order, bf16[32,80,128]{2,1,0:T(8,128)(2,1)} %pad_maximum_fusion.qb, bf16[8,16,4096]{2,1,0:T(8,128)(2,1)} %fusion.8.xb, ...), custom_call_target="tpu_custom_call" | custom-call | tf_op jit(solution)/shard_map/pallas_call | solution.py:508
  98.6 0.0 copy-start.1
  98.6 1.2 %copy.28 = bf16[4,32,2,8,128]{4,3,2,1,0:T(8,128)(2,1)S(1)} copy(bf16[4,32,2,8,128]{4,3,0,2,1:T(8,128)(2,1)} %bitcast.47) | data formatting | bytes 1048576 | tf_op jit(solution)/shard_map/transpose | solution.py:672
  99.8 1.0 reshape.310
  100.9 0.6 convert_multiply_fusion
  101.4 0.7 copy-done.2
  102.1 1.5 %fusion = bf16[128,4096]{1,0:T(8,128)(2,1)} fusion(f32[128,4096]{1,0:T(8,128)S(1)} %bitcast.38, bf16[128,4096]{1,0:T(8,128)(2,1)S(1)} %bitcast.43, s32[128]{0:T(128)S(1)} %add.112), kind=kOutput, calls=%fused_computation.1 | convolution fusion | flops 135282688 | bytes 4194816 | tf_op jit(solution)/shard_map/pb,bc->pc/dot_general | solution.py:678
  (7 shorter events, 0.0 us)
Async XLA Ops:
  0.6 1.2 %copy-start = (bf16[4,32,4096]{2,1,0:T(8,128)(2,1)S(1)}, bf16[4,32,4096]{2,1,0:T(8,128)(2,1)}, u32[]{:S(2)}) copy-start(bf16[4,32,4096]{2,1,0:T(8,128)(2,1)} %param.26) | copy-start | bytes 3145732
  98.6 2.3 %copy-start.1 = (bf16[4,32,4096]{2,1,0:T(8,128)(2,1)S(1)}, bf16[4,32,4096]{2,1,0:T(8,128)(2,1)}, u32[]{:S(2)}) copy-start(bf16[4,32,4096]{2,1,0:T(8,128)(2,1)} %param.27) | copy-start | bytes 3145732
  100.9 1.2 %copy-start.2 = (bf16[8,16,4096]{2,1,0:T(8,128)(2,1)S(1)}, bf16[8,16,4096]{2,1,0:T(8,128)(2,1)}, u32[]{:S(2)}) copy-start(bf16[8,16,4096]{2,1,0:T(8,128)(2,1)} %get-tuple-element.5) | copy-start | bytes 3145732

commit v6 on v5

--- a/solution.py
+++ b/solution.py
@@ -10,7 +10,7 @@
 
 HEAD_SIZE = 128
 BLOCK_ROWS = 16
-X_PARTS = 2
+X_PARTS = 4
 TILES_TOGETHER = 2
 EPSILON = 1e-06
 LOG2E = 1.4426950408889634
@@ -326,7 +326,7 @@
             lax.fori_loop(
                 portion * (half // chunk), (portion + 1) * (half // chunk), conv_chunk, 0
             )
-        if portion == 0:
+        if portion == X_PARTS - 2:
             for copies in x_copies:
                 for copy in copies:
                     copy.wait_send()
@@ -468,7 +468,7 @@
 
 
 def scan_chunk_of(block_width):
-    return min(512, block_width)
+    return min(256, block_width)
 
 
 def decode(

time: 104 us -> 99 us (0.952)
  Pallas kernels: 88.5 us -> 83.7 us
    pallas_call x1, Pallas kernels: 88.5 us -> 83.7 us  [decode(): pl.pallas_call(functools.partial(decode_kernel, kv_heads, q_rows, steps),...]
where the time goes in v6:
time: 99 us; the launch traced here: 98.7 us
  Pallas kernels  83.7 us (85%)
  local copies, waits for them, and re-layouts  6.91 us (7%)
  other arithmetic  4.49 us (5%)
  matrix products  2.9 us (3%)
    pallas_call x1, Pallas kernels, decode(): pl.pallas_call(functools.partial(decode_kernel, kv_heads, q_rows, steps),...  83.7 us
    unnamed x7, local copies, waits for them, and re-layouts  3.04 us

profile of v6, /device:TPU:0, one launch (start us, length us, event | category | flops | bytes accessed | tf_op | source)
XLA Modules:
  0.0 98.7 jit_solution(15358870726546061978)
XLA Ops:
  0.6 0.0 copy-start
  0.6 1.2 %copy-done = bf16[4,32,4096]{2,1,0:T(8,128)(2,1)S(1)} copy-done((bf16[4,32,4096]{2,1,0:T(8,128)(2,1)S(1)}, bf16[4,32,4096]{2,1,0:T(8,128)(2,1)}, u32[]{:S(2)}) %copy-start) | copy-done | bytes 1048600
  1.9 0.9 convert_reduce_fusion
  2.8 0.7 multiply_add_fusion.1
  3.4 0.7 select_reduce_fusion.order
  4.1 0.1 add_add_fusion
  4.2 0.1 add.112
  4.3 0.1 add.116
  4.3 0.1 add.117
  4.4 0.1 add.115
  4.5 0.7 fusion.5
  5.2 1.0 %reshape.305 = bf16[4,32,2,2,128]{4,3,2,1,0:T(2,128)(2,1)S(1)} reshape(bf16[4,32,2,256]{3,2,1,0:T(2,128)(2,1)} %param.19) | data formatting | bytes 262144 | tf_op jit(solution)/shard_map/reshape | solution.py:646
  6.2 0.2 copy.27
  6.4 1.1 %copy.29 = bf16[16,8,16,128]{3,2,1,0:T(8,128)(2,1)S(1)} copy(bf16[16,8,16,128]{3,1,2,0:T(8,128)(2,1)} %bitcast.46) | data formatting | bytes 1048576
  7.6 0.1 copy.26
  7.7 0.9 pad_maximum_fusion.qb
  8.6 1.5 %fusion.8.xb = bf16[8,16,4096]{2,1,0:T(8,128)(2,1)} fusion(bf16[128,4096,1]{1,0,2:T(8,128)(2,1)S(1)} %bitcast.36, s32[8,16]{1,0:T(8,128)S(1)} %multiply_add_fusion, s32[128]{0:T(128)S(1)} %add.112), kind=kOutput, calls=%fused_computation.14 | convolution fusion | flops 134234112 | bytes 2098176 | tf_op jit(solution)/shard_map/pb,pc->bc/dot_general | solution.py:639
  10.1 83.7 %shard_map.185 = (bf16[32,64,128]{2,1,0:T(8,128)(2,1)}, bf16[8,16,4096]{2,1,0:T(8,128)(2,1)}) custom-call(s32[8,32]{1,0:T(8,128)} %bitcast.51, s32[32]{0:T(128)} %lengths.1, s32[32]{0:T(128)} %select_reduce_fusion.order, bf16[32,80,128]{2,1,0:T(8,128)(2,1)} %pad_maximum_fusion.qb, bf16[8,16,4096]{2,1,0:T(8,128)(2,1)} %fusion.8.xb, ...), custom_call_target="tpu_custom_call" | custom-call | tf_op jit(solution)/shard_map/pallas_call | solution.py:508
  93.7 0.0 copy-start.1
  93.7 1.2 %copy.28 = bf16[4,32,2,8,128]{4,3,2,1,0:T(8,128)(2,1)S(1)} copy(bf16[4,32,2,8,128]{4,3,0,2,1:T(8,128)(2,1)} %bitcast.47) | data formatting | bytes 1048576 | tf_op jit(solution)/shard_map/transpose | solution.py:672
  95.0 1.0 %reshape.310 = bf16[4,32,2048]{2,1,0:T(8,128)(2,1)} reshape(bf16[4,32,2,8,128]{4,3,2,1,0:T(8,128)(2,1)S(1)} %copy.28) | data formatting | bytes 1048576 | tf_op jit(solution)/shard_map/reshape | solution.py:674
  96.0 0.6 convert_multiply_fusion
  96.5 0.7 copy-done.2
  97.2 1.5 %fusion = bf16[128,4096]{1,0:T(8,128)(2,1)} fusion(f32[128,4096]{1,0:T(8,128)S(1)} %bitcast.38, bf16[128,4096]{1,0:T(8,128)(2,1)S(1)} %bitcast.43, s32[128]{0:T(128)S(1)} %add.112), kind=kOutput, calls=%fused_computation.1 | convolution fusion | flops 135282688 | bytes 4194816 | tf_op jit(solution)/shard_map/pb,bc->pc/dot_general | solution.py:678
  (7 shorter events, 0.0 us)
Async XLA Ops:
  0.6 1.2 %copy-start = (bf16[4,32,4096]{2,1,0:T(8,128)(2,1)S(1)}, bf16[4,32,4096]{2,1,0:T(8,128)(2,1)}, u32[]{:S(2)}) copy-start(bf16[4,32,4096]{2,1,0:T(8,128)(2,1)} %param.26) | copy-start | bytes 3145732
  93.7 2.3 %copy-start.1 = (bf16[4,32,4096]{2,1,0:T(8,128)(2,1)S(1)}, bf16[4,32,4096]{2,1,0:T(8,128)(2,1)}, u32[]{:S(2)}) copy-start(bf16[4,32,4096]{2,1,0:T(8,128)(2,1)} %param.27) | copy-start | bytes 3145732
  96.0 1.2 %copy-start.2 = (bf16[8,16,4096]{2,1,0:T(8,128)(2,1)S(1)}, bf16[8,16,4096]{2,1,0:T(8,128)(2,1)}, u32[]{:S(2)}) copy-start(bf16[8,16,4096]{2,1,0:T(8,128)(2,1)} %get-tuple-element.5) | copy-start | bytes 3145732
